TPU v7x, 256 devices: a whole 4x4x8 slice. The times are simulated.
256 devices in a mesh: head: 8 (over y, core), ctx: 32 (over x, z).
Axes of the slice: x: 4, y: 4, z: 8, core: 2. Of those that a mesh axis runs over, the one named last changes fastest.
Arguments:
- queries: bfloat16 [12288, 5120], P('ctx', 'head'), may hold values from -150 to 150
- keys: bfloat16 [12288, 5120], P('ctx', 'head'), may hold values from -21.1 to 21.1
- values: bfloat16 [12288, 5120], P('ctx', 'head'), may hold values from -6 to 6
- grad_out: bfloat16 [12288, 5120], P('ctx', 'head'), may hold values from -192 to 192
- key_tiles: int32 [32, 6], replicated, may hold values from -1 to 31, as said below
- tile_slot: int32 [32], replicated, may hold values from 0 to 31, as said below
Outputs:
- grad_queries: bfloat16 [32, 384, 5120], P('ctx', 'head')
- grad_keys: bfloat16 [32, 384, 5120], P('ctx', 'head')
- grad_values: bfloat16 [32, 384, 5120], P('ctx', 'head')
Inputs may be any that keep to these rules, and one draw needn't show every extreme that they name: tile_slot[t] = t for every tile t (each storage block holds one tile). `key_tiles`: row t lists in increasing order tile t and other tiles within 3 of t, distinct; where all 7 tiles around t exist, exactly one tile other than t is left out, else all existing ones are listed and -1 fills the remaining entries.
All inputs are finite; a program needn't handle non-finite values.
Results may differ from a plain program's by a relative error of at most 0.01.
Values may be sent and summed in bfloat16 or wider, within the bound.
A program may use at most 128 MiB of HBM per device.

v0:
```python
import jax
import jax.numpy as jnp
from jax import lax
from jax.sharding import PartitionSpec as P

DH = 128
TILE = 384
REACH = 3


def passed_along(block, axis, distance):
    devices = range(lax.axis_size(axis))
    route = [(i - distance, i) for i in devices if i - distance in devices]
    return lax.ppermute(block, axis, route)


def shards(queries, keys, values, grad_out, key_tiles, tile_slot):
    rows, width = queries.shape
    local_tiles = rows // TILE
    heads = width // DH
    depth = (REACH + local_tiles - 1) // local_tiles
    total_tiles = key_tiles.shape[0]
    position = lax.axis_index("ctx")
    scale = DH ** (-0.5)
    paired = jnp.stack((keys, values))
    nearby = {0: paired}
    for offset in range(-depth, depth + 1):
        if offset != 0:
            nearby[offset] = passed_along(paired, "ctx", -offset)
    count = (2 * depth + 1) * local_tiles
    window = jnp.concatenate([nearby[offset] for offset in range(-depth, depth + 1)], axis=1)
    window = window.reshape(2, count, TILE, width)
    first_slot = (position - depth) * local_tiles
    my_slots = position * local_tiles + jnp.arange(local_tiles, dtype=jnp.int32)
    every_tile = jnp.arange(total_tiles, dtype=jnp.int32)
    owned = tile_slot[None, :] == my_slots[:, None]
    listed = jnp.sum(jnp.where(owned[:, :, None], key_tiles[None, :, :], 0), axis=1)
    usable = listed >= 0
    matches = listed[:, :, None] == every_tile[None, None, :]
    listed_slots = jnp.sum(jnp.where(matches, tile_slot[None, None, :], 0), axis=2)
    local_index = jnp.clip(listed_slots - first_slot, 0, count - 1)
    chosen_keys = window[0][local_index]
    chosen_values = window[1][local_index]
    placement = (
        (local_index[:, :, None] == jnp.arange(count, dtype=jnp.int32)[None, None, :])
        & usable[:, :, None]
    ).astype(jnp.float32)
    query_blocks = queries.reshape(local_tiles, TILE, width)
    grad_blocks = grad_out.reshape(local_tiles, TILE, width)
    highest = lax.Precision.HIGHEST

    def forward_part(head):
        start = head * DH
        query_head = lax.dynamic_slice_in_dim(query_blocks, start, DH, 2)
        grad_head = lax.dynamic_slice_in_dim(grad_blocks, start, DH, 2)
        key_head = lax.dynamic_slice_in_dim(chosen_keys, start, DH, 3)
        value_head = lax.dynamic_slice_in_dim(chosen_values, start, DH, 3)
        scores = (
            jnp.einsum("tqd,tjkd->tqjk", query_head, key_head, preferred_element_type=jnp.float32)
            * scale
        )
        scores = jnp.where(usable[:, None, :, None], scores, -1e30)
        summit = jnp.max(scores, axis=(2, 3), keepdims=True)
        expon = jnp.exp(scores - summit)
        total = jnp.sum(expon, axis=(2, 3), keepdims=True)
        probs = expon / total
        dprobs = jnp.einsum(
            "tqd,tjkd->tqjk", grad_head, value_head, preferred_element_type=jnp.float32
        )
        delta = jnp.sum(probs * dprobs, axis=(2, 3), keepdims=True)
        dscores = (probs * (dprobs - delta)).astype(jnp.bfloat16)
        grad_query = (
            jnp.einsum("tqjk,tjkd->tqd", dscores, key_head, preferred_element_type=jnp.float32)
            * scale
        )
        return (query_head, grad_head, probs, dscores, grad_query, summit, total, delta)

    def per_head(carry, head):
        query_head, grad_head, probs, dscores, grad_query, summit, total, delta = forward_part(head)
        probs_low = probs.astype(jnp.bfloat16)
        key_part = (
            jnp.einsum("tqjk,tqd->tjkd", dscores, query_head, preferred_element_type=jnp.float32)
            * scale
        )
        value_part = jnp.einsum(
            "tqjk,tqd->tjkd", probs_low, grad_head, preferred_element_type=jnp.float32
        )
        key_sum = jnp.einsum("tjn,tjkd->nkd", placement, key_part, precision=highest)
        value_sum = jnp.einsum("tjn,tjkd->nkd", placement, value_part, precision=highest)
        return (carry, (grad_query, key_sum, value_sum))

    unused, (grad_query, key_sum, value_sum) = lax.scan(
        per_head, jnp.zeros((), jnp.float32), jnp.arange(heads, dtype=jnp.int32)
    )
    grad_query = grad_query.transpose(1, 2, 0, 3).reshape(local_tiles, TILE, width)
    key_sum = key_sum.transpose(1, 2, 0, 3).reshape(count, TILE, width)
    value_sum = value_sum.transpose(1, 2, 0, 3).reshape(count, TILE, width)
    stacked = jnp.stack((key_sum, value_sum)).reshape(2, 2 * depth + 1, local_tiles, TILE, width)
    gathered = stacked[:, depth]
    for offset in range(-depth, depth + 1):
        if offset != 0:
            gathered = gathered + passed_along(
                stacked[:, depth + offset].astype(jnp.bfloat16), "ctx", offset
            ).astype(jnp.float32)
    results = jnp.stack(
        (
            grad_query.astype(jnp.bfloat16),
            gathered[0].astype(jnp.bfloat16),
            gathered[1].astype(jnp.bfloat16),
        )
    )
    moved = lax.all_to_all(results, "head", split_axis=2, concat_axis=3, tiled=True)
    return (moved[0], moved[1], moved[2])


def solution(mesh):
    in_specs = (P("ctx", "head"), P("ctx", "head"), P("ctx", "head"), P("ctx", "head"), P(), P())
    out_specs = (P("ctx", "head", None), P("ctx", "head", None), P("ctx", "head", None))
    return jax.shard_map(shards, mesh=mesh, in_specs=in_specs, out_specs=out_specs, check_vma=False)
```

profile of v0, /device:TPU:38, one launch (start us, length us, event | category | flops | bytes accessed | tf_op | source)
XLA Modules:
  0.0 479.7 jit_solution(2030278678108551349)
XLA Ops:
  2.0 7.7 %collective-permute-start = (bf16[2,384,640]{2,1,0:T(8,128)(2,1)S(1)}, bf16[2,384,640]{2,1,0:T(8,128)(2,1)}, u32[]{:S(2)}, u32[]{:S(2)}) collective-permute-start(bf16[2,384,640]{2,1,0:T(8,128)(2,1)S(1)} %pad_maximum_fusion.1), channel_id=1, source_target_pairs={{0,3},{1,4},{2,5},{3,6},{4,7},{5,8},{6,9},{7,10},{8,11},{9,12},{10... | collective-permute-start | bytes 2949128 | tf_op jit(solution)/shard_map/ppermute | solution.py:14
  17.8 5.2 %collective-permute-start.1 = (bf16[2,384,640]{2,1,0:T(8,128)(2,1)S(1)}, bf16[2,384,640]{2,1,0:T(8,128)(2,1)}, u32[]{:S(2)}, u32[]{:S(2)}) collective-permute-start(bf16[2,384,640]{2,1,0:T(8,128)(2,1)S(1)} %pad_maximum_fusion.1), channel_id=1, source_target_pairs={{0,2},{1,3},{2,4},{3,5},{4,6},{5,7},{6,8},{7,9},{8,10},{9,11},{10,... | collective-permute-start | bytes 2949128 | tf_op jit(solution)/shard_map/ppermute | solution.py:14
  25.5 49.0 %collective-permute-done = bf16[2,384,640]{2,1,0:T(8,128)(2,1)} collective-permute-done((bf16[2,384,640]{2,1,0:T(8,128)(2,1)S(1)}, bf16[2,384,640]{2,1,0:T(8,128)(2,1)}, u32[]{:S(2)}, u32[]{:S(2)}) %collective-permute-start) | collective-permute-done | bytes 983072 | tf_op jit(solution)/shard_map/ppermute | solution.py:14
  74.5 3.3 collective-permute-start.4
  79.6 57.6 %collective-permute-done.1 = bf16[2,384,640]{2,1,0:T(8,128)(2,1)} collective-permute-done((bf16[2,384,640]{2,1,0:T(8,128)(2,1)S(1)}, bf16[2,384,640]{2,1,0:T(8,128)(2,1)}, u32[]{:S(2)}, u32[]{:S(2)}) %collective-permute-start.1) | collective-permute-done | bytes 983072 | tf_op jit(solution)/shard_map/ppermute | solution.py:14
  145.4 4.7 gather_fusion.1
  152.8 134.8 %while.15 = (s32[]{:T(128)}, bf16[5,1,384,128]{2,3,0,1:T(8,128)(2,1)}, f32[5,7,384,128]{2,3,0,1:T(8,128)}, f32[5,7,384,128]{2,3,0,1:T(8,128)}, pred[1,6]{1,0:T(4...) while((s32[]{:T(128)}, ...), condition=%wide.region_6.7_spmd.clone, body=%wide.region_2.6_spmd.clone.sunk | while | flops 1204518016 | bytes 51235972 | solution.py:92
  158.5 3.3 fusion.97
  161.8 3.0 copy.125
  176.2 3.5 constant_dynamic-update-slice_fusion.13
  185.4 3.3 fusion.97
  188.7 3.0 copy.125
  203.2 3.6 constant_dynamic-update-slice_fusion.13
  212.4 3.3 fusion.97
  230.1 3.6 constant_dynamic-update-slice_fusion.13
  239.4 3.3 fusion.97
  257.1 3.5 constant_dynamic-update-slice_fusion.13
  266.3 3.3 fusion.97
  284.0 3.5 constant_dynamic-update-slice_fusion.13
  287.5 8.7 %fusion.62 = bf16[2,7,1,384,640]{3,4,1,0,2:T(8,128)(2,1)} fusion(f32[1,7,384,640]{2,3,1,0:T(8,128)} %bitcast.168, f32[1,7,384,640]{2,3,1,0:T(8,128)} %bitcast.170), kind=kLoop, calls=%fused_computation.90 | loop fusion | flops 3440640 | bytes 20643840 | tf_op jit(solution)/shard_map/convert.7
  296.3 4.6 slice_bitcast_fusion.6
  300.9 5.0 %collective-permute-start.6 = (bf16[2,1,384,640]{2,3,0,1:T(8,128)(2,1)S(1)}, bf16[2,1,384,640]{2,3,0,1:T(8,128)(2,1)S(1)}, u32[]{:S(2)}, u32[]{:S(2)}) collective-permute-start(bf16[2,1,384,640]{2,3,0,1:T(8,128)(2,1)S(1)} %get-tuple-element.125), channel_id=1, source_target_pairs={{3,0},{4,1},{5,2},{6,3},{7,4},{8,5},{9,6},{10,7},{11,8},{12,9},{13... | collective-permute-start | bytes 2949128 | tf_op jit(solution)/shard_map/ppermute | solution.py:14
  307.9 4.1 collective-permute-start.8
  312.0 5.5 %collective-permute-start.7 = (bf16[2,1,384,640]{2,3,0,1:T(8,128)(2,1)}, bf16[2,1,384,640]{2,3,0,1:T(8,128)(2,1)}, u32[]{:S(2)}, u32[]{:S(2)}) collective-permute-start(bf16[2,1,384,640]{2,3,0,1:T(8,128)(2,1)} %get-tuple-element.128), channel_id=1, source_target_pairs={{2,0},{3,1},{4,2},{5,3},{6,4},{7,5},{8,6},{9,7},{10,8},{11,9},{12,... | collective-permute-start | bytes 2949128 | tf_op jit(solution)/shard_map/ppermute | solution.py:14
  319.4 48.1 %collective-permute-done.6 = bf16[2,1,384,640]{2,3,0,1:T(8,128)(2,1)S(1)} collective-permute-done((bf16[2,1,384,640]{2,3,0,1:T(8,128)(2,1)S(1)}, bf16[2,1,384,640]{2,3,0,1:T(8,128)(2,1)S(1)}, u32[]{:S(2)}, u32[]{:S(2)}) %collective-permute-start.6) | collective-permute-done | bytes 983072 | tf_op jit(solution)/shard_map/ppermute | solution.py:14
  367.5 4.4 collective-permute-start.10
  371.9 11.0 %maximum_bitcast_fusion = f32[2,7,1,384,640]{3,4,1,0,2:T(8,128)} fusion(f32[1,7,384,640]{2,3,1,0:T(8,128)} %bitcast.169, f32[1,7,384,640]{2,3,1,0:T(8,128)} %bitcast.171), kind=kLoop, calls=%fused_computation.56 | loop fusion | flops 3440640 | bytes 27525120 | tf_op jit(solution)/shard_map/reshape | solution.py:98
  382.9 7.9 %collective-permute-done.8 = bf16[2,1,384,640]{2,3,0,1:T(8,128)(2,1)} collective-permute-done((bf16[2,1,384,640]{2,3,0,1:T(8,128)(2,1)}, bf16[2,1,384,640]{2,3,0,1:T(8,128)(2,1)}, u32[]{:S(2)}, u32[]{:S(2)}) %collective-permute-start.8) | collective-permute-done | bytes 983072 | tf_op jit(solution)/shard_map/ppermute | solution.py:14
  390.8 42.0 %collective-permute-done.7 = bf16[2,1,384,640]{2,3,0,1:T(8,128)(2,1)} collective-permute-done((bf16[2,1,384,640]{2,3,0,1:T(8,128)(2,1)}, bf16[2,1,384,640]{2,3,0,1:T(8,128)(2,1)}, u32[]{:S(2)}, u32[]{:S(2)}) %collective-permute-start.7) | collective-permute-done | bytes 983072 | tf_op jit(solution)/shard_map/ppermute | solution.py:14
  432.9 7.0 %collective-permute-done.10 = bf16[2,1,384,640]{2,3,0,1:T(8,128)(2,1)} collective-permute-done((bf16[2,1,384,640]{2,3,0,1:T(8,128)(2,1)S(1)}, bf16[2,1,384,640]{2,3,0,1:T(8,128)(2,1)}, u32[]{:S(2)}, u32[]{:S(2)}) %collective-permute-start.10) | collective-permute-done | bytes 983072 | tf_op jit(solution)/shard_map/ppermute | solution.py:14
  439.9 3.8 fusion.58
  445.7 30.3 %all_to_all.15 = bf16[3,1,384,640]{3,0,1,2:T(4,128)(2,1)S(1)} all-to-all(bf16[3,1,384,640]{3,0,1,2:T(4,128)(2,1)S(1)} %copy.87), channel_id=1, replica_groups=mesh['head'=8,'ctx'=32] {'head'}, dimensions={2} | all-to-all | bytes 2949120 | tf_op jit(solution)/shard_map/all_to_all | solution.py:112
  (150 shorter events, 125.1 us)
Async XLA Ops:
  0.6 139.4 %copy-start = (bf16[384,640]{1,0:T(8,128)(2,1)S(1)}, bf16[384,640]{1,0:T(8,128)(2,1)}, u32[]{:S(2)}) copy-start(bf16[384,640]{1,0:T(8,128)(2,1)} %param.10) | copy-start | bytes 1474564
  0.6 139.4 %copy-start.1 = (bf16[384,640]{1,0:T(8,128)(2,1)S(1)}, bf16[384,640]{1,0:T(8,128)(2,1)}, u32[]{:S(2)}) copy-start(bf16[384,640]{1,0:T(8,128)(2,1)} %param.9) | copy-start | bytes 1474564
  2.0 72.5 %collective-permute-start = (bf16[2,384,640]{2,1,0:T(8,128)(2,1)S(1)}, bf16[2,384,640]{2,1,0:T(8,128)(2,1)}, u32[]{:S(2)}, u32[]{:S(2)}) collective-permute-start(bf16[2,384,640]{2,1,0:T(8,128)(2,1)S(1)} %pad_maximum_fusion.1), channel_id=1, source_target_pairs={{0,3},{1,4},{2,5},{3,6},{4,7},{5,8},{6,9},{7,10},{8,11},{9,12},{10... | collective-permute-start | bytes 2949128 | tf_op jit(solution)/shard_map/ppermute | solution.py:14
  9.8 133.1 %collective-permute-start.5 = (bf16[2,384,640]{2,1,0:T(8,128)(2,1)S(1)}, bf16[2,384,640]{2,1,0:T(8,128)(2,1)S(1)}, u32[]{:S(2)}, u32[]{:S(2)}) collective-permute-start(bf16[2,384,640]{2,1,0:T(8,128)(2,1)S(1)} %pad_maximum_fusion.1), channel_id=1, source_target_pairs={{3,0},{4,1},{5,2},{6,3},{7,4},{8,5},{9,6},{10,7},{11,8},{12,9},{13... | collective-permute-start | bytes 2949128 | tf_op jit(solution)/shard_map/ppermute | solution.py:14
  12.0 128.2 %collective-permute-start.3 = (bf16[2,384,640]{2,1,0:T(8,128)(2,1)S(1)}, bf16[2,384,640]{2,1,0:T(8,128)(2,1)}, u32[]{:S(2)}, u32[]{:S(2)}) collective-permute-start(bf16[2,384,640]{2,1,0:T(8,128)(2,1)S(1)} %pad_maximum_fusion.1), channel_id=1, source_target_pairs={{1,0},{2,1},{3,2},{4,3},{5,4},{6,5},{7,6},{8,7},{9,8},{10,9},{11,1... | collective-permute-start | bytes 2949128 | tf_op jit(solution)/shard_map/ppermute | solution.py:14
  14.9 123.7 %collective-permute-start.2 = (bf16[2,384,640]{2,1,0:T(8,128)(2,1)S(1)}, bf16[2,384,640]{2,1,0:T(8,128)(2,1)}, u32[]{:S(2)}, u32[]{:S(2)}) collective-permute-start(bf16[2,384,640]{2,1,0:T(8,128)(2,1)S(1)} %pad_maximum_fusion.1), channel_id=1, source_target_pairs={{0,1},{1,2},{2,3},{3,4},{4,5},{5,6},{6,7},{7,8},{8,9},{9,10},{10,1... | collective-permute-start | bytes 2949128 | tf_op jit(solution)/shard_map/ppermute | solution.py:14
  17.8 119.4 %collective-permute-start.1 = (bf16[2,384,640]{2,1,0:T(8,128)(2,1)S(1)}, bf16[2,384,640]{2,1,0:T(8,128)(2,1)}, u32[]{:S(2)}, u32[]{:S(2)}) collective-permute-start(bf16[2,384,640]{2,1,0:T(8,128)(2,1)S(1)} %pad_maximum_fusion.1), channel_id=1, source_target_pairs={{0,2},{1,3},{2,4},{3,5},{4,6},{5,7},{6,8},{7,9},{8,10},{9,11},{10,... | collective-permute-start | bytes 2949128 | tf_op jit(solution)/shard_map/ppermute | solution.py:14
  74.5 67.1 %collective-permute-start.4 = (bf16[2,384,640]{2,1,0:T(8,128)(2,1)S(1)}, bf16[2,384,640]{2,1,0:T(8,128)(2,1)}, u32[]{:S(2)}, u32[]{:S(2)}) collective-permute-start(bf16[2,384,640]{2,1,0:T(8,128)(2,1)S(1)} %pad_maximum_fusion.1), channel_id=1, source_target_pairs={{2,0},{3,1},{4,2},{5,3},{6,4},{7,5},{8,6},{9,7},{10,8},{11,9},{12,... | collective-permute-start | bytes 2949128 | tf_op jit(solution)/shard_map/ppermute | solution.py:14
  156.5 1.9 copy-start.3
  168.3 4.1 copy-start.4
  174.6 5.1 %copy-start.6 = (s32[5]{0:T(128)S(1)}, s32[5]{0:T(128)}, u32[]{:S(2)}) copy-start(s32[5]{0:T(128)} %copy-done.5) | copy-start | bytes 64 | tf_op jit(solution)/shard_map/while
  183.5 1.9 copy-start.3
  195.3 4.1 copy-start.4
  201.6 5.2 %copy-start.6 = (s32[5]{0:T(128)S(1)}, s32[5]{0:T(128)}, u32[]{:S(2)}) copy-start(s32[5]{0:T(128)} %copy-done.5) | copy-start | bytes 64 | tf_op jit(solution)/shard_map/while
  210.5 1.9 copy-start.3
  222.3 4.1 copy-start.4
  228.6 5.1 %copy-start.6 = (s32[5]{0:T(128)S(1)}, s32[5]{0:T(128)}, u32[]{:S(2)}) copy-start(s32[5]{0:T(128)} %copy-done.5) | copy-start | bytes 64 | tf_op jit(solution)/shard_map/while
  233.7 1.2 copy-start.5
  237.5 1.9 copy-start.3
  249.3 4.1 copy-start.4
  255.5 5.1 %copy-start.6 = (s32[5]{0:T(128)S(1)}, s32[5]{0:T(128)}, u32[]{:S(2)}) copy-start(s32[5]{0:T(128)} %copy-done.5) | copy-start | bytes 64 | tf_op jit(solution)/shard_map/while
  260.6 1.2 copy-start.5
  264.4 1.9 copy-start.3
  276.2 4.1 copy-start.4
  282.4 5.1 %copy-start.6 = (s32[5]{0:T(128)S(1)}, s32[5]{0:T(128)}, u32[]{:S(2)}) copy-start(s32[5]{0:T(128)} %copy-done.5) | copy-start | bytes 64 | tf_op jit(solution)/shard_map/while
  300.9 66.5 %collective-permute-start.6 = (bf16[2,1,384,640]{2,3,0,1:T(8,128)(2,1)S(1)}, bf16[2,1,384,640]{2,3,0,1:T(8,128)(2,1)S(1)}, u32[]{:S(2)}, u32[]{:S(2)}) collective-permute-start(bf16[2,1,384,640]{2,3,0,1:T(8,128)(2,1)S(1)} %get-tuple-element.125), channel_id=1, source_target_pairs={{3,0},{4,1},{5,2},{6,3},{7,4},{8,5},{9,6},{10,7},{11,8},{12,9},{13... | collective-permute-start | bytes 2949128 | tf_op jit(solution)/shard_map/ppermute | solution.py:14
  306.0 77.0 %collective-permute-start.9 = (bf16[2,1,384,640]{2,3,0,1:T(8,128)(2,1)}, bf16[2,1,384,640]{2,3,0,1:T(8,128)(2,1)}, u32[]{:S(2)}, u32[]{:S(2)}) collective-permute-start(bf16[2,1,384,640]{2,3,0,1:T(8,128)(2,1)} %get-tuple-element.126), channel_id=1, source_target_pairs={{0,1},{1,2},{2,3},{3,4},{4,5},{5,6},{6,7},{7,8},{8,9},{9,10},{10,1... | collective-permute-start | bytes 2949128 | tf_op jit(solution)/shard_map/ppermute | solution.py:14
  307.9 83.0 %collective-permute-start.8 = (bf16[2,1,384,640]{2,3,0,1:T(8,128)(2,1)}, bf16[2,1,384,640]{2,3,0,1:T(8,128)(2,1)}, u32[]{:S(2)}, u32[]{:S(2)}) collective-permute-start(bf16[2,1,384,640]{2,3,0,1:T(8,128)(2,1)} %get-tuple-element.127), channel_id=1, source_target_pairs={{1,0},{2,1},{3,2},{4,3},{5,4},{6,5},{7,6},{8,7},{9,8},{10,9},{11,1... | collective-permute-start | bytes 2949128 | tf_op jit(solution)/shard_map/ppermute | solution.py:14
  312.0 120.9 %collective-permute-start.7 = (bf16[2,1,384,640]{2,3,0,1:T(8,128)(2,1)}, bf16[2,1,384,640]{2,3,0,1:T(8,128)(2,1)}, u32[]{:S(2)}, u32[]{:S(2)}) collective-permute-start(bf16[2,1,384,640]{2,3,0,1:T(8,128)(2,1)} %get-tuple-element.128), channel_id=1, source_target_pairs={{2,0},{3,1},{4,2},{5,3},{6,4},{7,5},{8,6},{9,7},{10,8},{11,9},{12,... | collective-permute-start | bytes 2949128 | tf_op jit(solution)/shard_map/ppermute | solution.py:14
  317.5 115.4 %collective-permute-start.11 = (bf16[2,1,384,640]{2,3,0,1:T(8,128)(2,1)S(1)}, bf16[2,1,384,640]{2,3,0,1:T(8,128)(2,1)}, u32[]{:S(2)}, u32[]{:S(2)}) collective-permute-start(bf16[2,1,384,640]{2,3,0,1:T(8,128)(2,1)S(1)} %get-tuple-element.129), channel_id=1, source_target_pairs={{0,3},{1,4},{2,5},{3,6},{4,7},{5,8},{6,9},{7,10},{8,11},{9,12},{10... | collective-permute-start | bytes 2949128 | tf_op jit(solution)/shard_map/ppermute | solution.py:14
  367.5 72.4 %collective-permute-start.10 = (bf16[2,1,384,640]{2,3,0,1:T(8,128)(2,1)S(1)}, bf16[2,1,384,640]{2,3,0,1:T(8,128)(2,1)}, u32[]{:S(2)}, u32[]{:S(2)}) collective-permute-start(bf16[2,1,384,640]{2,3,0,1:T(8,128)(2,1)S(1)} %get-tuple-element.130), channel_id=1, source_target_pairs={{0,2},{1,3},{2,4},{3,5},{4,6},{5,7},{6,8},{7,9},{8,10},{9,11},{10,... | collective-permute-start | bytes 2949128 | tf_op jit(solution)/shard_map/ppermute | solution.py:14
  382.9 60.7 %copy-start.2 = (bf16[5,1,384,128]{2,3,0,1:T(8,128)(2,1)S(1)}, bf16[5,1,384,128]{2,3,0,1:T(8,128)(2,1)}, u32[]{:S(2)}) copy-start(bf16[5,1,384,128]{2,3,0,1:T(8,128)(2,1)} %get-tuple-element.62) | copy-start | bytes 1474564
  (3 other events, 3.5 us)
where the time goes:
time: 481 us; the launch traced here: 480 us
  waiting for transfers between devices  212 us (44%)
  local copies, waits for them, and re-layouts  74.2 us (15%)
  matrix products  73.4 us (15%)
  starting transfers between devices  47.2 us (10%)
  other arithmetic  38.7 us (8%)
  blocking collectives  30.3 us (6%)
    ppermute x12, waiting for transfers between devices, passed_along(): return lax.ppermute(block, axis, route)  212 us
    ppermute x12, starting transfers between devices, passed_along(): return lax.ppermute(block, axis, route)  47.2 us
    dynamic_update_slice x25, local copies, waits for them, and re-layouts, shards(): lax.scan(per_head, jnp.zeros((), jnp.float32), jnp.arange(heads, dtype=jn...  44.5 us
    all_to_all x1, blocking collectives, shards(): lax.all_to_all(results, 'head', split_axis=2, concat_axis=3, tiled=True)  30.3 us
    dot_general x5, matrix products, per_head(): jnp.einsum('tjn,tjkd->nkd', placement, value_part, precision=highest)  16.6 us
    another operation x4, other arithmetic  12.5 us
    dot_general x5, matrix products, forward_part(): jnp.einsum('tqd,tjkd->tqjk', grad_head, value_head, preferred_element_typ...  11.3 us
    reshape x1, other arithmetic, shards(): jnp.stack((key_sum, value_sum))  11 us
  transfers between devices with their start and end apart: 12, of which 6 were waited for; matrix products, arithmetic and copies ran while one was open for 4% of the time, Pallas kernels for 0%

commit v1 on v0

v1 whole, which is shorter than its diff:
```python
import functools
import math

import jax
import jax.numpy as jnp
from jax import lax
from jax.experimental import pallas as pl
from jax.experimental.pallas import tpu as pltpu
from jax.sharding import PartitionSpec as P

DH = 128
REACH = 3
SPAN = 2 * REACH + 1
LOW = -1e30
MESH = pl.DeviceIdType.MESH
NT = (((1,), (1,)), ((), ()))

LAG_A = 2
LAG_C = 3
LAG_B = 3


def kernel(
    n_ctx, n_head, heads, tile,
    tiles_ref, q_hbm, k_hbm, v_hbm, g_hbm,
    dq_hbm, dk_hbm, dv_hbm,
    win, kv, expon, dprob, summit, stat_out, stat_in, res_out, res_in, bias,
    part, hop_out, hop_in, block_q, block_k, block_v,
    load_sem, kv_sem, win_send, win_recv, stat_send, stat_recv, res_send, res_recv,
    hop_send, hop_recv, out_send, out_recv, own_sem,
):
    me = lax.axis_index("ctx")
    lane = lax.axis_index("head")
    rows = tile // n_head
    thirds = tile // 128
    scale = DH ** -0.5
    log_scale = scale * math.log2(math.e)

    def at(offset):
        return lax.rem(me + offset + n_ctx, n_ctx)

    barrier = pltpu.get_barrier_semaphore()
    for offset in range(-REACH, REACH + 1):
        if offset != 0:
            pl.semaphore_signal(
                barrier, inc=1, device_id={"ctx": at(offset)}, device_id_type=MESH
            )
    for shift in range(1, n_head):
        pl.semaphore_signal(
            barrier, inc=1, device_id={"head": lax.rem(lane + shift, n_head)},
            device_id_type=MESH,
        )

    def columns(h):
        return pl.ds(pl.multiple_of(h * DH, DH), DH)

    def own_loads(h):
        return [
            pltpu.make_async_copy(q_hbm.at[:, columns(h)], win.at[REACH, h, 0], load_sem.at[h, 0]),
            pltpu.make_async_copy(g_hbm.at[:, columns(h)], win.at[REACH, h, 1], load_sem.at[h, 1]),
        ]

    def kv_loads(h):
        return [
            pltpu.make_async_copy(k_hbm.at[:, columns(h)], kv.at[h, 0], kv_sem.at[h, 0]),
            pltpu.make_async_copy(v_hbm.at[:, columns(h)], kv.at[h, 1], kv_sem.at[h, 1]),
        ]

    @pl.loop(0, heads)
    def _(h):
        for copy in own_loads(h) + kv_loads(h):
            copy.start()

    for p in range(SPAN):
        other = at(p - REACH)
        mine = jnp.zeros((), jnp.bool_)
        theirs = jnp.zeros((), jnp.bool_)
        for j in range(tiles_ref.shape[1]):
            mine = jnp.logical_or(mine, tiles_ref[me, j] == other)
            theirs = jnp.logical_or(theirs, tiles_ref[other, j] == me)
        bias[0, p] = jnp.where(mine, 0.0, LOW)
        bias[1, p] = jnp.where(theirs, 0.0, LOW)

    pl.semaphore_wait(barrier, 2 * REACH + n_head - 1)

    def relay(direction, distance, h):
        step = -1 if direction == 0 else 1
        source = REACH + step * distance
        return pltpu.make_async_remote_copy(
            src_ref=win.at[source, h],
            dst_ref=win.at[source + step, h],
            send_sem=win_send.at[direction, distance, h],
            recv_sem=win_recv.at[direction, distance, h],
            device_id={"ctx": at(-step)},
            device_id_type=MESH,
        )

    def hop(direction, distance, h):
        return pltpu.make_async_remote_copy(
            src_ref=hop_out.at[direction, distance, h],
            dst_ref=hop_in.at[direction, distance, h],
            send_sem=hop_send.at[direction, distance, h],
            recv_sem=hop_recv.at[direction, distance, h],
            device_id={"ctx": at(-1 if direction == 0 else 1)},
            device_id_type=MESH,
        )

    def stat_copy(p, h):
        return pltpu.make_async_remote_copy(
            src_ref=stat_out.at[h, p],
            dst_ref=stat_in.at[h, 2 * REACH - p],
            send_sem=stat_send.at[h, p],
            recv_sem=stat_recv.at[h, 2 * REACH - p],
            device_id={"ctx": at(p - REACH)},
            device_id_type=MESH,
        )

    def res_copy(p, h):
        return pltpu.make_async_remote_copy(
            src_ref=res_out.at[h],
            dst_ref=res_in.at[h, 2 * REACH - p],
            send_sem=res_send.at[h, p],
            recv_sem=res_recv.at[h, 2 * REACH - p],
            device_id={"ctx": at(p - REACH)},
            device_id_type=MESH,
        )

    def spread(block, target, kind, h):
        place = columns(lane * heads + h)
        pltpu.make_async_copy(
            block.at[h, pl.ds(pl.multiple_of(lane * rows, 16), rows), :],
            target.at[0, :, place],
            own_sem.at[kind, h],
        ).start()

        @pl.loop(1, n_head)
        def _(shift):
            peer = lax.rem(lane + shift, n_head)
            pltpu.make_async_remote_copy(
                src_ref=block.at[h, pl.ds(pl.multiple_of(peer * rows, 16), rows), :],
                dst_ref=target.at[0, :, place],
                send_sem=out_send.at[kind],
                recv_sem=out_recv.at[kind],
                device_id={"head": peer},
                device_id_type=MESH,
            ).start()

    def wide(ref, start):
        return jnp.concatenate([ref[start + j : start + j + 1, :] for j in range(thirds)], axis=1)

    def first_pass(h):
        slot = lax.rem(h, 2)
        for copy in kv_loads(h):
            copy.wait()

        @pl.loop(0, SPAN)
        def _(p):
            scores = lax.dot_general(
                kv[h, 0], win[p, h, 0], NT, preferred_element_type=jnp.float32
            ) * log_scale
            top = jnp.max(scores, axis=0, keepdims=True)
            weights = jnp.exp2(scores - top)
            total = jnp.sum(weights, axis=0, keepdims=True)
            dp = lax.dot_general(kv[h, 1], win[p, h, 1], NT, preferred_element_type=jnp.float32)
            mean = jnp.sum(weights * dp, axis=0, keepdims=True) / total
            expon[slot, p] = weights
            dprob[slot, p] = dp
            summit[slot, p] = top
            level = top + jnp.log2(total)
            for j in range(thirds):
                stat_out[h, p, j : j + 1, :] = level[:, j * 128 : (j + 1) * 128]
                stat_out[h, p, thirds + j : thirds + j + 1, :] = mean[:, j * 128 : (j + 1) * 128]

            @pl.when(p != REACH)
            def _():
                stat_copy(p, h).start()

    def combine(h):
        levels = []
        for p in range(SPAN):
            if p != REACH:
                stat_copy(2 * REACH - p, h).wait_recv()
            source = stat_out if p == REACH else stat_in
            levels.append(source[h, p, 0:thirds, :] + bias[0, p])
        top = functools.reduce(jnp.maximum, levels)
        total = jnp.zeros_like(top)
        delta = jnp.zeros_like(top)
        for p in range(SPAN):
            source = stat_out if p == REACH else stat_in
            weight = jnp.exp2(levels[p] - top)
            total = total + weight
            delta = delta + weight * source[h, p, thirds : 2 * thirds, :]
        level = top + jnp.log2(total)
        delta = delta / total
        res_out[h, 0:thirds, :] = level
        res_out[h, thirds : 2 * thirds, :] = delta
        res_in[h, REACH, 0:thirds, :] = level
        res_in[h, REACH, thirds : 2 * thirds, :] = delta
        for p in range(SPAN):
            if p != REACH:
                res_copy(p, h).start()

    def second_pass(h):
        slot = lax.rem(h, 2)
        keys_turned = kv[h, 0].T

        def body(p, carry):
            dk, dv = carry

            @pl.when(p != REACH)
            def _():
                res_copy(2 * REACH - p, h).wait_recv()

            result = res_in.at[h, p]
            factor = jnp.exp2(summit[slot, p] + bias[1, p] - wide(result, 0))
            delta = wide(result, thirds)
            probs = expon[slot, p] * factor
            dscores = (probs * (dprob[slot, p] - delta)).astype(jnp.bfloat16)
            dv = dv + jnp.dot(
                probs.astype(jnp.bfloat16), win[p, h, 1], preferred_element_type=jnp.float32
            )
            dk = dk + jnp.dot(dscores, win[p, h, 0], preferred_element_type=jnp.float32)
            part[h, p] = (
                jnp.dot(keys_turned, dscores, preferred_element_type=jnp.float32) * scale
            )
            return dk, dv

        start = (jnp.zeros((tile, DH), jnp.float32), jnp.zeros((tile, DH), jnp.float32))
        dk, dv = lax.fori_loop(0, SPAN, body, start)
        for direction, p in ((0, 0), (1, 2 * REACH)):
            hop_out[direction, 0, h] = part[h, p].astype(jnp.bfloat16)
            hop(direction, 0, h).start()
        block_k[h] = (dk * scale).astype(jnp.bfloat16)
        block_v[h] = dv.astype(jnp.bfloat16)
        spread(block_k, dk_hbm, 1, h)
        spread(block_v, dv_hbm, 2, h)

    def pass_on(distance, h):
        for direction, p in ((0, distance), (1, 2 * REACH - distance)):
            hop(direction, distance - 1, h).wait_recv()
            hop_out[direction, distance, h] = (
                part[h, p] + hop_in[direction, distance - 1, h].astype(jnp.float32)
            ).astype(jnp.bfloat16)
            hop(direction, distance, h).start()

    def finish(h):
        total = part[h, REACH]
        for direction in range(2):
            hop(direction, REACH - 1, h).wait_recv()
            total = total + hop_in[direction, REACH - 1, h].astype(jnp.float32)
        block_q[h] = total.T.astype(jnp.bfloat16)
        spread(block_q, dq_hbm, 0, h)

    def send_own(h):
        for copy in own_loads(h):
            copy.wait()
        for direction in range(2):
            relay(direction, 0, h).start()

    send_own(0)

    def during(lag, s, action):
        @pl.when(jnp.logical_and(s >= lag, s < heads + lag))
        def _():
            action(s - lag)

    def forward(distance, h):
        for direction in range(2):
            relay(direction, distance - 1, h).wait_recv()
            if distance < REACH:
                relay(direction, distance, h).start()

    @pl.loop(0, heads + LAG_B + REACH)
    def _(s):
        @pl.when(s < heads - 1)
        def _():
            send_own(s + 1)

        during(0, s, functools.partial(forward, 1))
        during(1, s, functools.partial(forward, 2))
        during(LAG_B + 1, s, functools.partial(pass_on, 1))
        during(LAG_B + 2, s, functools.partial(pass_on, 2))
        during(LAG_B + 3, s, finish)
        during(LAG_C, s, combine)
        during(2, s, functools.partial(forward, 3))
        during(LAG_A, s, first_pass)
        during(LAG_B, s, second_pass)

    @pl.loop(0, heads)
    def _(h):
        for direction in range(2):
            for distance in range(REACH):
                relay(direction, distance, h).wait_send()
                hop(direction, distance, h).wait_send()
        for p in range(SPAN):
            if p != REACH:
                stat_copy(p, h).wait_send()
                res_copy(p, h).wait_send()
        for kind, (block, target) in enumerate(
            ((block_q, dq_hbm), (block_k, dk_hbm), (block_v, dv_hbm))
        ):
            pltpu.make_async_copy(
                block.at[h, pl.ds(pl.multiple_of(lane * rows, 16), rows), :],
                target.at[0, :, columns(lane * heads + h)],
                own_sem.at[kind, h],
            ).wait()

    for kind, target in enumerate((dq_hbm, dk_hbm, dv_hbm)):
        others = target.at[0, :, pl.ds(0, (n_head - 1) * heads * DH)]
        pltpu.make_async_copy(others, others, out_send.at[kind]).wait()
        pltpu.make_async_copy(others, others, out_recv.at[kind]).wait()


def shards(queries, keys, values, grad_out, key_tiles, tile_slot):
    tile, width = queries.shape
    heads = width // DH
    n_ctx = lax.axis_size("ctx")
    n_head = lax.axis_size("head")
    rows = tile // n_head
    bf16, f32 = jnp.bfloat16, jnp.float32
    dma = pltpu.SemaphoreType.DMA
    out = jax.ShapeDtypeStruct((1, rows, n_head * width), bf16)
    pairs = heads * SPAN * tile * tile
    return pl.pallas_call(
        functools.partial(kernel, n_ctx, n_head, heads, tile),
        out_shape=(out, out, out),
        in_specs=[pl.BlockSpec(memory_space=pltpu.SMEM)] + [pl.BlockSpec(memory_space=pl.ANY)] * 4,
        out_specs=tuple([pl.BlockSpec(memory_space=pl.ANY)] * 3),
        scratch_shapes=[
            pltpu.VMEM((SPAN, heads, 2, tile, DH), bf16),
            pltpu.VMEM((heads, 2, tile, DH), bf16),
            pltpu.VMEM((2, SPAN, tile, tile), f32),
            pltpu.VMEM((2, SPAN, tile, tile), f32),
            pltpu.VMEM((2, SPAN, 1, tile), f32),
            pltpu.VMEM((heads, SPAN, 8, 128), f32),
            pltpu.VMEM((heads, SPAN, 8, 128), f32),
            pltpu.VMEM((heads, 8, 128), f32),
            pltpu.VMEM((heads, SPAN, 8, 128), f32),
            pltpu.SMEM((2, SPAN), f32),
            pltpu.VMEM((heads, SPAN, DH, tile), f32),
            pltpu.VMEM((2, REACH, heads, DH, tile), bf16),
            pltpu.VMEM((2, REACH, heads, DH, tile), bf16),
            pltpu.VMEM((heads, tile, DH), bf16),
            pltpu.VMEM((heads, tile, DH), bf16),
            pltpu.VMEM((heads, tile, DH), bf16),
            dma((heads, 2)),
            dma((heads, 2)),
            dma((2, REACH, heads)),
            dma((2, REACH, heads)),
            dma((heads, SPAN)),
            dma((heads, SPAN)),
            dma((heads, SPAN)),
            dma((heads, SPAN)),
            dma((2, REACH, heads)),
            dma((2, REACH, heads)),
            dma((3,)),
            dma((3,)),
            dma((3, heads)),
        ],
        compiler_params=pltpu.CompilerParams(
            collective_id=0, has_side_effects=True, vmem_limit_bytes=60 * 1024 * 1024
        ),
        cost_estimate=pl.CostEstimate(
            flops=10 * pairs * DH, bytes_accessed=8 * tile * width * 2, transcendentals=pairs
        ),
    )(key_tiles, queries, keys, values, grad_out)


def solution(mesh):
    in_specs = (P("ctx", "head"), P("ctx", "head"), P("ctx", "head"), P("ctx", "head"), P(), P())
    out_specs = (P("ctx", "head", None), P("ctx", "head", None), P("ctx", "head", None))
    return jax.shard_map(shards, mesh=mesh, in_specs=in_specs, out_specs=out_specs, check_vma=False)
```

time: 481 us -> 161 us (0.33)
  the two profiles are of different devices: /device:TPU:38 before, /device:TPU:1 now
where the time goes in v1:
time: 161 us; the launch traced here: 160 us
  Pallas kernels  155 us (96%)
  local copies, waits for them, and re-layouts  5.26 us (3%)
    pallas_call x1, Pallas kernels, shards(): pl.pallas_call(functools.partial(kernel, n_ctx, n_head, heads, tile), out...  155 us
    unnamed x8, local copies, waits for them, and re-layouts  5.26 us

profile of v1, /device:TPU:1, one launch (start us, length us, event | category | flops | bytes accessed | tf_op | source)
XLA Modules:
  0.0 160.5 jit_solution(4111528986434845195)
XLA Ops:
  0.6 1.4 copy.8.tiles_ref
  2.0 154.6 %shard_map.76 = (bf16[1,48,5120]{2,1,0:T(8,128)(2,1)}, bf16[1,48,5120]{2,1,0:T(8,128)(2,1)}, bf16[1,48,5120]{2,1,0:T(8,128)(2,1)}) custom-call(s32[32,6]{1,0:T(8,128)} %copy.8.tiles_ref, bf16[384,640]{1,0:T(8,128)(2,1)} %q_hbm.1, bf16[384,640]{1,0:T(8,128)(2,1)} %k_hbm.1, bf16[384,640]{1,0:T(8,128)(2,1)} %v_hbm.1, bf16[384,640]{1,0:T(8,128)(2,1)} %g_hbm.1), custom_call_target="tpu_custom_call" | custom-call | flops 6606028800 | bytes 3932160 | tf_op jit(solution)/shard_map/pallas_call | solution.py:324
  156.6 0.0 copy-start.1
  156.6 1.9 %copy.12 = bf16[1,48,5120]{2,1,0:T(8,128)(2,1)} copy(bf16[1,48,5120]{2,1,0:T(8,128)(2,1)} %get-tuple-element.6) | data formatting | bytes 983040
  158.5 0.0 copy-done.1
  158.5 0.0 copy-start
  158.5 0.8 copy.13
  159.3 0.4 copy-done
  159.7 0.8 copy.14
Async XLA Ops:
  156.6 1.9 %copy-start.1 = (bf16[1,48,5120]{2,1,0:T(8,128)(2,1)S(1)}, bf16[1,48,5120]{2,1,0:T(8,128)(2,1)}, u32[]{:S(2)}) copy-start(bf16[1,48,5120]{2,1,0:T(8,128)(2,1)} %get-tuple-element.7) | copy-start | bytes 1474564
  158.5 1.2 copy-start

commit v2 on v1

--- a/solution.py
+++ b/solution.py
@@ -17,17 +17,17 @@
 
 LAG_A = 2
 LAG_C = 3
-LAG_B = 3
+LAG_B = 4
 
 
 def kernel(
     n_ctx, n_head, heads, tile,
-    tiles_ref, q_hbm, k_hbm, v_hbm, g_hbm,
+    tiles_hbm, q_hbm, k_hbm, v_hbm, g_hbm,
     dq_hbm, dk_hbm, dv_hbm,
     win, kv, expon, dprob, summit, stat_out, stat_in, res_out, res_in, bias,
     part, hop_out, hop_in, block_q, block_k, block_v,
     load_sem, kv_sem, win_send, win_recv, stat_send, stat_recv, res_send, res_recv,
-    hop_send, hop_recv, out_send, out_recv, own_sem,
+    hop_send, hop_recv, out_send, out_recv, own_sem, tiles_ref, tiles_sem,
 ):
     me = lax.axis_index("ctx")
     lane = lax.axis_index("head")
@@ -38,6 +38,9 @@
 
     def at(offset):
         return lax.rem(me + offset + n_ctx, n_ctx)
+
+    tiles_copy = pltpu.make_async_copy(tiles_hbm, tiles_ref, tiles_sem)
+    tiles_copy.start()
 
     barrier = pltpu.get_barrier_semaphore()
     for offset in range(-REACH, REACH + 1):
@@ -71,13 +74,14 @@
         for copy in own_loads(h) + kv_loads(h):
             copy.start()
 
+    tiles_copy.wait()
     for p in range(SPAN):
         other = at(p - REACH)
         mine = jnp.zeros((), jnp.bool_)
         theirs = jnp.zeros((), jnp.bool_)
-        for j in range(tiles_ref.shape[1]):
-            mine = jnp.logical_or(mine, tiles_ref[me, j] == other)
-            theirs = jnp.logical_or(theirs, tiles_ref[other, j] == me)
+        for j in range(tiles_ref.shape[0]):
+            mine = jnp.logical_or(mine, tiles_ref[j, me] == other)
+            theirs = jnp.logical_or(theirs, tiles_ref[j, other] == me)
         bias[0, p] = jnp.where(mine, 0.0, LOW)
         bias[1, p] = jnp.where(theirs, 0.0, LOW)
 
@@ -148,13 +152,12 @@
     def wide(ref, start):
         return jnp.concatenate([ref[start + j : start + j + 1, :] for j in range(thirds)], axis=1)
 
-    def first_pass(h):
-        slot = lax.rem(h, 2)
-        for copy in kv_loads(h):
-            copy.wait()
-
-        @pl.loop(0, SPAN)
-        def _(p):
+    def first_pass(first, stride, count, h):
+        slot = lax.rem(h, LAG_B - LAG_A)
+
+        @pl.loop(0, count)
+        def _(i):
+            p = first + stride * i
             scores = lax.dot_general(
                 kv[h, 0], win[p, h, 0], NT, preferred_element_type=jnp.float32
             ) * log_scale
@@ -174,6 +177,10 @@
             @pl.when(p != REACH)
             def _():
                 stat_copy(p, h).start()
+
+    def wait_keys(h):
+        for copy in kv_loads(h):
+            copy.wait()
 
     def combine(h):
         levels = []
@@ -201,7 +208,7 @@
                 res_copy(p, h).start()
 
     def second_pass(h):
-        slot = lax.rem(h, 2)
+        slot = lax.rem(h, LAG_B - LAG_A)
         keys_turned = kv[h, 0].T
 
         def body(p, carry):
@@ -272,19 +279,22 @@
 
     @pl.loop(0, heads + LAG_B + REACH)
     def _(s):
+        during(LAG_B + 1, s, functools.partial(pass_on, 1))
+        during(2, s, functools.partial(forward, 2))
+        during(LAG_B, s, second_pass)
+        during(LAG_C, s, combine)
+        during(1, s, functools.partial(forward, 1))
+        during(LAG_A, s, wait_keys)
+        during(LAG_A, s, functools.partial(first_pass, 1, 1, SPAN - 2))
+        during(LAG_B + 2, s, functools.partial(pass_on, 2))
+        during(LAG_B + 3, s, finish)
+
         @pl.when(s < heads - 1)
         def _():
             send_own(s + 1)
 
-        during(0, s, functools.partial(forward, 1))
-        during(1, s, functools.partial(forward, 2))
-        during(LAG_B + 1, s, functools.partial(pass_on, 1))
-        during(LAG_B + 2, s, functools.partial(pass_on, 2))
-        during(LAG_B + 3, s, finish)
-        during(LAG_C, s, combine)
-        during(2, s, functools.partial(forward, 3))
-        during(LAG_A, s, first_pass)
-        during(LAG_B, s, second_pass)
+        during(LAG_A, s, functools.partial(forward, 3))
+        during(LAG_A, s, functools.partial(first_pass, 0, SPAN - 1, 2))
 
     @pl.loop(0, heads)
     def _(h):
@@ -311,31 +321,43 @@
         pltpu.make_async_copy(others, others, out_recv.at[kind]).wait()
 
 
+def copy_kernel(a, b, c, a_out, b_out, c_out, sems):
+    copies = [
+        pltpu.make_async_copy(source, target, sems.at[i])
+        for i, (source, target) in enumerate(((a, a_out), (b, b_out), (c, c_out)))
+    ]
+    for copy in copies:
+        copy.start()
+    for copy in copies:
+        copy.wait()
+
+
 def shards(queries, keys, values, grad_out, key_tiles, tile_slot):
     tile, width = queries.shape
     heads = width // DH
     n_ctx = lax.axis_size("ctx")
     n_head = lax.axis_size("head")
     rows = tile // n_head
+    thirds = tile // 128
     bf16, f32 = jnp.bfloat16, jnp.float32
     dma = pltpu.SemaphoreType.DMA
     out = jax.ShapeDtypeStruct((1, rows, n_head * width), bf16)
     pairs = heads * SPAN * tile * tile
-    return pl.pallas_call(
+    grads = pl.pallas_call(
         functools.partial(kernel, n_ctx, n_head, heads, tile),
         out_shape=(out, out, out),
-        in_specs=[pl.BlockSpec(memory_space=pltpu.SMEM)] + [pl.BlockSpec(memory_space=pl.ANY)] * 4,
-        out_specs=tuple([pl.BlockSpec(memory_space=pl.ANY)] * 3),
+        in_specs=[pl.BlockSpec(memory_space=pl.ANY)] * 5,
+        out_specs=tuple([pl.BlockSpec(memory_space=pltpu.VMEM)] * 3),
         scratch_shapes=[
             pltpu.VMEM((SPAN, heads, 2, tile, DH), bf16),
             pltpu.VMEM((heads, 2, tile, DH), bf16),
-            pltpu.VMEM((2, SPAN, tile, tile), f32),
-            pltpu.VMEM((2, SPAN, tile, tile), f32),
-            pltpu.VMEM((2, SPAN, 1, tile), f32),
-            pltpu.VMEM((heads, SPAN, 8, 128), f32),
-            pltpu.VMEM((heads, SPAN, 8, 128), f32),
-            pltpu.VMEM((heads, 8, 128), f32),
-            pltpu.VMEM((heads, SPAN, 8, 128), f32),
+            pltpu.VMEM((LAG_B - LAG_A, SPAN, tile, tile), f32),
+            pltpu.VMEM((LAG_B - LAG_A, SPAN, tile, tile), f32),
+            pltpu.VMEM((LAG_B - LAG_A, SPAN, 1, tile), f32),
+            pltpu.VMEM((heads, SPAN, 2 * thirds, 128), f32),
+            pltpu.VMEM((heads, SPAN, 2 * thirds, 128), f32),
+            pltpu.VMEM((heads, 2 * thirds, 128), f32),
+            pltpu.VMEM((heads, SPAN, 2 * thirds, 128), f32),
             pltpu.SMEM((2, SPAN), f32),
             pltpu.VMEM((heads, SPAN, DH, tile), f32),
             pltpu.VMEM((2, REACH, heads, DH, tile), bf16),
@@ -356,6 +378,8 @@
             dma((3,)),
             dma((3,)),
             dma((3, heads)),
+            pltpu.SMEM(key_tiles.shape[::-1], jnp.int32),
+            dma,
         ],
         compiler_params=pltpu.CompilerParams(
             collective_id=0, has_side_effects=True, vmem_limit_bytes=60 * 1024 * 1024
@@ -363,7 +387,14 @@
         cost_estimate=pl.CostEstimate(
             flops=10 * pairs * DH, bytes_accessed=8 * tile * width * 2, transcendentals=pairs
         ),
-    )(key_tiles, queries, keys, values, grad_out)
+    )(key_tiles.T, queries, keys, values, grad_out)
+    return pl.pallas_call(
+        copy_kernel,
+        out_shape=(out, out, out),
+        in_specs=[pl.BlockSpec(memory_space=pltpu.VMEM)] * 3,
+        out_specs=tuple([pl.BlockSpec(memory_space=pl.ANY)] * 3),
+        scratch_shapes=[dma((3,))],
+    )(*grads)
 
 
 def solution(mesh):

time: 161 us -> 132 us (0.82)
  Pallas kernels: 155 us -> 132 us
  local copies, waits for them, and re-layouts: 5.26 us -> 0 us
    pallas_call x1, Pallas kernels: 155 us -> 129 us  [shards(): pl.pallas_call(functools.partial(kernel, n_ctx, n_head, heads, tile), out...]
    unnamed x8 -> x0, local copies, waits for them, and re-layouts: 5.26 us -> none
    pallas_call x0 -> x1, Pallas kernels: none -> 2.45 us  [shards(): pl.pallas_call(copy_kernel, out_shape=(out, out, out), in_specs=[pl.Block...]
where the time goes in v2:
time: 132 us
  Pallas kernels  132 us (100%)
    pallas_call x1, Pallas kernels, shards(): pl.pallas_call(functools.partial(kernel, n_ctx, n_head, heads, tile), out...  129 us

profile of v2, /device:TPU:1, one launch (start us, length us, event | category | flops | bytes accessed | tf_op | source)
XLA Modules:
  0.0 132.2 jit_solution(5742529533749644048)
XLA Ops:
  0.6 129.1 %shard_map.76 = (bf16[1,48,5120]{2,1,0:T(8,128)(2,1)}, bf16[1,48,5120]{2,1,0:T(8,128)(2,1)}, bf16[1,48,5120]{2,1,0:T(8,128)(2,1)}) custom-call(s32[6,32]{1,0:T(8,128)} %bitcast.1, bf16[384,640]{1,0:T(8,128)(2,1)} %q_hbm.1, bf16[384,640]{1,0:T(8,128)(2,1)} %k_hbm.1, bf16[384,640]{1,0:T(8,128)(2,1)} %v_hbm.1, bf16[384,640]{1,0:T(8,128)(2,1)} %g_hbm.1), custom_call_target="tpu_custom_call" | custom-call | flops 6606028800 | bytes 3932160 | tf_op jit(solution)/shard_map/pallas_call | solution.py:346
  129.7 2.5 %shard_map.77 = (bf16[1,48,5120]{2,1,0:T(8,128)(2,1)}, bf16[1,48,5120]{2,1,0:T(8,128)(2,1)}, bf16[1,48,5120]{2,1,0:T(8,128)(2,1)}) custom-call(bf16[1,48,5120]{2,1,0:T(8,128)(2,1)} %get-tuple-element.6.a, bf16[1,48,5120]{2,1,0:T(8,128)(2,1)} %get-tuple-element.7.b, bf16[1,48,5120]{2,1,0:T(8,128)(2,1)} %get-tuple-element.8.c), custom_call_target="tpu_custom_call" | custom-call | tf_op jit(solution)/shard_map/pallas_call | solution.py:391

commit v3 on v0

v3 whole, which is shorter than its diff:
```python
import functools
import math

import jax
import jax.numpy as jnp
from jax import lax
from jax.experimental import pallas as pl
from jax.experimental.pallas import tpu as pltpu
from jax.sharding import PartitionSpec as P

DH = 128
REACH = 3
SPAN = 2 * REACH + 1
LOW = -1e30
MESH = pl.DeviceIdType.MESH
NT = (((1,), (1,)), ((), ()))
RING = 8
RUN = RING // 2
WIDE = RUN + 2 * REACH


def kernel(
    n_ctx, n_head, heads, tile,
    tiles_hbm, q_hbm, k_hbm, v_hbm, g_hbm,
    dq_out, dk_out, dv_out,
    tiles_ref, bias, wide_bias,
    wwin, wkv, wexp, wdp, wtop, wstat, stat_out, stat_in, wres, wdq, edge_out, edge_in, made,
    win, kv, expon, dprob, summit, lone_out, lone_in, res_out, res_in, part, hop_out, hop_in,
    block_q, block_k, block_v,
    tiles_sem, load_sem, in_send, in_recv, side_send, side_recv, wstat_send, wstat_recv,
    wres_send, wres_recv, edge_send, edge_recv, home_send, home_recv,
    win_send, win_recv, stat_send, stat_recv, res_send, res_recv, hop_send, hop_recv,
    out_send, out_recv, own_sem,
):
    me = lax.axis_index("ctx")
    lane = lax.axis_index("head")
    rows = tile // n_head
    thirds = tile // 128
    scale = DH ** -0.5
    log_scale = scale * math.log2(math.e)
    last = heads - 1
    core = lax.rem(lane, 2)
    z = lax.rem(me, RING)
    zl = lax.rem(z, RUN)
    zh = z // RUN
    chip_lane = lane - core
    line = me - z
    first_tile = RUN * (2 * (me // RING) + core)
    stays = zh == core

    def peer(i):
        return (chip_lane + zh, line + RUN * core + i)

    sides = (
        (chip_lane + 1 - core, lax.rem(me - (1 - core) * RING + n_ctx, n_ctx)),
        (chip_lane + 1 - core, lax.rem(me + core * RING, n_ctx)),
    )

    def at(offset):
        return (lane, lax.rem(me + offset + n_ctx, n_ctx))

    def lane_at(shift):
        return (lax.rem(lane + shift, n_head), me)

    tiles_copy = pltpu.make_async_copy(tiles_hbm, tiles_ref, tiles_sem)
    tiles_copy.start()

    barrier = pltpu.get_barrier_semaphore()

    def greet(device):
        pl.semaphore_signal(barrier, inc=1, device_id=device, device_id_type=MESH)

    for i in range(RUN):
        @pl.when(jnp.logical_not(jnp.logical_and(stays, zl == i)))
        def _():
            greet(peer(i))
    for device in sides:
        greet(device)
    for offset in range(-REACH, REACH + 1):
        if offset != 0:
            greet(at(offset))
    for shift in range(1, n_head):
        greet(lane_at(shift))

    def columns(h):
        return pl.ds(pl.multiple_of(h * DH, DH), DH)

    loads = [
        pltpu.make_async_copy(source.at[:, columns(last)], target, load_sem.at[i])
        for i, (source, target) in enumerate((
            (q_hbm, win.at[REACH, 0]), (g_hbm, win.at[REACH, 1]),
            (k_hbm, kv.at[0]), (v_hbm, kv.at[1]),
        ))
    ]
    for copy in loads:
        copy.start()

    def landing(a, j):
        return wwin.at[REACH + a, j] if j < 2 else wkv.at[a, j - 2]

    sources = (q_hbm, g_hbm, k_hbm, v_hbm)

    def in_copy(r, j):
        i = lax.rem(zl + r, RUN)
        return pltpu.make_async_remote_copy(
            src_ref=sources[j].at[:, columns(i)],
            dst_ref=landing(zl, j),
            send_sem=in_send.at[r, j],
            recv_sem=in_recv.at[zl, j],
            device_id=peer(i),
            device_id_type=MESH,
        )

    def in_wait(a, j):
        pltpu.make_async_remote_copy(
            src_ref=sources[j].at[:, columns(a)],
            dst_ref=landing(a, j),
            send_sem=in_send.at[0, j],
            recv_sem=in_recv.at[a, j],
            device_id=peer(a),
            device_id_type=MESH,
        ).wait_recv()

    tiles_copy.wait()

    def listed(query_tile, key_tile):
        found = jnp.zeros((), jnp.bool_)
        for j in range(tiles_ref.shape[0]):
            found = jnp.logical_or(found, tiles_ref[j, query_tile] == key_tile)
        return jnp.where(found, 0.0, LOW)

    pl.semaphore_wait(
        barrier, 2 + 2 * REACH + n_head - 1 + RUN - jnp.where(stays, 1, 0).astype(jnp.int32)
    )

    for r, j in [(r, j) for pair in ((0, 1), (2, 3)) for r in range(RUN) for j in pair]:
        if True:
            if r > 0:
                in_copy(r, j).start()
            else:
                @pl.when(stays)
                def _():
                    pltpu.make_async_copy(
                        sources[j].at[:, columns(zl)], landing(zl, j), in_recv.at[zl, j]
                    ).start()

                @pl.when(jnp.logical_not(stays))
                def _():
                    in_copy(0, j).start()

    def relay(direction, distance):
        step = -1 if direction == 0 else 1
        source = REACH + step * distance
        return pltpu.make_async_remote_copy(
            src_ref=win.at[source],
            dst_ref=win.at[source + step],
            send_sem=win_send.at[direction, distance],
            recv_sem=win_recv.at[direction, distance],
            device_id=at(-step),
            device_id_type=MESH,
        )

    def forward(distance):
        for direction in range(2):
            relay(direction, distance - 1).wait_recv()
            if distance < REACH:
                relay(direction, distance).start()

    def hop(direction, distance):
        return pltpu.make_async_remote_copy(
            src_ref=hop_out.at[direction, distance],
            dst_ref=hop_in.at[direction, distance],
            send_sem=hop_send.at[direction, distance],
            recv_sem=hop_recv.at[direction, distance],
            device_id=at(-1 if direction == 0 else 1),
            device_id_type=MESH,
        )

    def stat_copy(p):
        return pltpu.make_async_remote_copy(
            src_ref=lone_out.at[p],
            dst_ref=lone_in.at[2 * REACH - p],
            send_sem=stat_send.at[p],
            recv_sem=stat_recv.at[2 * REACH - p],
            device_id=at(p - REACH),
            device_id_type=MESH,
        )

    def res_copy(p):
        return pltpu.make_async_remote_copy(
            src_ref=res_out,
            dst_ref=res_in.at[2 * REACH - p],
            send_sem=res_send.at[p],
            recv_sem=res_recv.at[2 * REACH - p],
            device_id=at(p - REACH),
            device_id_type=MESH,
        )

    def side_copy(side, a):
        shift = RUN if side == 0 else -RUN
        slot = a if side == 0 else a - 1
        return pltpu.make_async_remote_copy(
            src_ref=wwin.at[REACH + a],
            dst_ref=wwin.at[REACH + a + shift],
            send_sem=side_send.at[side, slot],
            recv_sem=side_recv.at[side, slot],
            device_id=sides[side],
            device_id_type=MESH,
        )

    def wstat_copy(side):
        return pltpu.make_async_remote_copy(
            src_ref=stat_out.at[side],
            dst_ref=stat_in.at[1 - side],
            send_sem=wstat_send.at[side],
            recv_sem=wstat_recv.at[1 - side],
            device_id=sides[side],
            device_id_type=MESH,
        )

    def wres_copy(side):
        return pltpu.make_async_remote_copy(
            src_ref=wres.at[pl.ds(REACH + side, REACH)],
            dst_ref=wres.at[pl.ds(REACH + RUN if side == 0 else 0, REACH)],
            send_sem=wres_send.at[side],
            recv_sem=wres_recv.at[1 - side],
            device_id=sides[side],
            device_id_type=MESH,
        )

    def edge_copy(side):
        return pltpu.make_async_remote_copy(
            src_ref=edge_out.at[side],
            dst_ref=edge_in.at[1 - side],
            send_sem=edge_send.at[side],
            recv_sem=edge_recv.at[1 - side],
            device_id=sides[side],
            device_id_type=MESH,
        )

    blocks = (block_q, block_k, block_v)
    targets = (dq_out, dk_out, dv_out)

    def home_copy(kind, i):
        return pltpu.make_async_remote_copy(
            src_ref=made.at[kind, i],
            dst_ref=blocks[kind].at[zl],
            send_sem=home_send.at[kind, i],
            recv_sem=home_recv.at[kind, zl],
            device_id=peer(i),
            device_id_type=MESH,
        )

    def home_local(kind, i):
        return pltpu.make_async_copy(
            made.at[kind, i], blocks[kind].at[zl], home_recv.at[kind, zl]
        )

    def go_home(kind, i):
        mine = jnp.logical_and(stays, zl == i)

        @pl.when(mine)
        def _():
            home_local(kind, i).start()

        @pl.when(jnp.logical_not(mine))
        def _():
            home_copy(kind, i).start()

    def own_part(kind, h):
        return pltpu.make_async_copy(
            blocks[kind].at[h, pl.ds(pl.multiple_of(lane * rows, 16), rows), :],
            targets[kind].at[0, :, columns(lane * heads + h)],
            own_sem.at[kind, h],
        )

    def spread(kind, h):
        own_part(kind, h).start()

        @pl.loop(1, n_head)
        def _(shift):
            device = lane_at(shift)
            pltpu.make_async_remote_copy(
                src_ref=blocks[kind].at[h, pl.ds(pl.multiple_of(device[0] * rows, 16), rows), :],
                dst_ref=targets[kind].at[0, :, columns(lane * heads + h)],
                send_sem=out_send.at[kind],
                recv_sem=out_recv.at[kind],
                device_id=device,
                device_id_type=MESH,
            ).start()

    def arrived(kind, h):
        pltpu.make_async_remote_copy(
            src_ref=made.at[kind, 0],
            dst_ref=blocks[kind].at[h],
            send_sem=home_send.at[kind, 0],
            recv_sem=home_recv.at[kind, h],
            device_id=peer(h),
            device_id_type=MESH,
        ).wait_recv()

    def wide(ref, start):
        return jnp.concatenate([ref[start + j : start + j + 1, :] for j in range(thirds)], axis=1)

    def score(key, value, query, grad, weights_ref, dp_ref, top_ref, stat_ref):
        scores = lax.dot_general(
            key[...], query[...], NT, preferred_element_type=jnp.float32
        ) * log_scale
        top = jnp.max(scores, axis=0, keepdims=True)
        weights = jnp.exp2(scores - top)
        total = jnp.sum(weights, axis=0, keepdims=True)
        dp = lax.dot_general(value[...], grad[...], NT, preferred_element_type=jnp.float32)
        mean = jnp.sum(weights * dp, axis=0, keepdims=True) / total
        weights_ref[...] = weights
        dp_ref[...] = dp
        top_ref[...] = top
        level = top + jnp.log2(total)
        for j in range(thirds):
            stat_ref[j : j + 1, :] = level[:, j * 128 : (j + 1) * 128]
            stat_ref[thirds + j : thirds + j + 1, :] = mean[:, j * 128 : (j + 1) * 128]

    def merge(parts):
        top = functools.reduce(jnp.maximum, [level for level, _ in parts])
        total = jnp.zeros_like(top)
        mean = jnp.zeros_like(top)
        for level, value in parts:
            weight = jnp.exp2(level - top)
            total = total + weight
            mean = mean + weight * value
        return top + jnp.log2(total), mean / total

    def put(ref, pair):
        ref[0:thirds, :] = pair[0]
        ref[thirds : 2 * thirds, :] = pair[1]

    def gradients(weights_ref, dp_ref, top_ref, offset, result, query, grad, turned):
        factor = jnp.exp2(top_ref[...] + offset - wide(result, 0))
        probs = weights_ref[...] * factor
        dscores = (probs * (dp_ref[...] - wide(result, thirds))).astype(jnp.bfloat16)
        dv = jnp.dot(probs.astype(jnp.bfloat16), grad[...], preferred_element_type=jnp.float32)
        dk = jnp.dot(dscores, query[...], preferred_element_type=jnp.float32)
        return dk, dv, jnp.dot(turned, dscores, preferred_element_type=jnp.float32)

    def wide_score(i, p):
        o = p - i
        score(
            wkv.at[i, 0], wkv.at[i, 1], wwin.at[p, 0], wwin.at[p, 1],
            wexp.at[i, o], wdp.at[i, o], wtop.at[i, o], wstat.at[i, o],
        )

    def local_parts(p):
        return [
            (
                wstat[i, p - i, 0:thirds, :] + wide_bias[i, p - i],
                wstat[i, p - i, thirds : 2 * thirds, :],
            )
            for i in range(RUN)
            if 0 <= p - i < SPAN
        ]

    def wide_gradients(i):
        turned = wkv[i, 0].T

        def body(o, carry):
            p = i + o
            dk, dv, dq = gradients(
                wexp.at[i, o], wdp.at[i, o], wtop.at[i, o], wide_bias[i, o], wres.at[p],
                wwin.at[p, 0], wwin.at[p, 1], turned,
            )
            wdq[p] = wdq[p] + dq
            return carry[0] + dk, carry[1] + dv

        start = (jnp.zeros((tile, DH), jnp.float32), jnp.zeros((tile, DH), jnp.float32))
        dk, dv = lax.fori_loop(0, SPAN, body, start)
        made[1, i] = (dk * scale).astype(jnp.bfloat16)
        made[2, i] = dv.astype(jnp.bfloat16)
        go_home(1, i)
        go_home(2, i)

    def send_edge(side):
        for i in range(REACH):
            edge_out[side, i] = wdq[i if side == 0 else REACH + RUN + i].astype(jnp.bfloat16)
        edge_copy(side).start()

    def lone_score(first, stride, count):
        @pl.loop(0, count)
        def _(i):
            p = first + stride * i
            score(
                kv.at[0], kv.at[1], win.at[p, 0], win.at[p, 1],
                expon.at[p], dprob.at[p], summit.at[p], lone_out.at[p],
            )

            @pl.when(p != REACH)
            def _():
                stat_copy(p).start()

    def lone_combine():
        parts = []
        for p in range(SPAN):
            if p != REACH:
                stat_copy(2 * REACH - p).wait_recv()
            source = lone_out if p == REACH else lone_in
            parts.append(
                (source[p, 0:thirds, :] + bias[0, p], source[p, thirds : 2 * thirds, :])
            )
        pair = merge(parts)
        put(res_out, pair)
        put(res_in.at[REACH], pair)
        for p in range(SPAN):
            if p != REACH:
                res_copy(p).start()

    def lone_gradients():
        turned = kv[0].T

        def body(p, carry):
            @pl.when(p != REACH)
            def _():
                res_copy(2 * REACH - p).wait_recv()

            dk, dv, dq = gradients(
                expon.at[p], dprob.at[p], summit.at[p], bias[1, p], res_in.at[p],
                win.at[p, 0], win.at[p, 1], turned,
            )
            part[p] = dq
            return carry[0] + dk, carry[1] + dv

        start = (jnp.zeros((tile, DH), jnp.float32), jnp.zeros((tile, DH), jnp.float32))
        dk, dv = lax.fori_loop(0, SPAN, body, start)
        for direction, p in ((0, 0), (1, 2 * REACH)):
            hop_out[direction, 0] = part[p].astype(jnp.bfloat16)
            hop(direction, 0).start()
        block_k[last] = (dk * scale).astype(jnp.bfloat16)
        block_v[last] = dv.astype(jnp.bfloat16)
        spread(1, last)
        spread(2, last)

    def pass_on(distance):
        for direction, p in ((0, distance), (1, 2 * REACH - distance)):
            hop(direction, distance - 1).wait_recv()
            hop_out[direction, distance] = (
                part[p] + hop_in[direction, distance - 1].astype(jnp.float32)
            ).astype(jnp.bfloat16)
            hop(direction, distance).start()

    def lone_finish():
        total = part[REACH]
        for direction in range(2):
            hop(direction, REACH - 1).wait_recv()
            total = total + hop_in[direction, REACH - 1].astype(jnp.float32)
        block_q[last] = (total * scale).T.astype(jnp.bfloat16)
        spread(0, last)

    for copy in loads:
        copy.wait()
    for direction in range(2):
        relay(direction, 0).start()

    wdq[...] = jnp.zeros_like(wdq)
    for p in range(SPAN):
        other = lax.rem(me + p - REACH + n_ctx, n_ctx)
        bias[0, p] = listed(me, other)
        bias[1, p] = listed(other, me)
    for i in range(RUN):
        for o in range(SPAN):
            query_tile = lax.rem(first_tile + i + o - REACH + n_ctx, n_ctx)
            wide_bias[i, o] = listed(query_tile, first_tile + i)

    def received(r):
        return lax.rem(zl - r + RUN, RUN)

    for r in range(RUN):
        newest = received(r)
        for j in range(2):
            in_wait(newest, j)

        @pl.when(newest < REACH)
        def _():
            side_copy(0, newest).start()

        @pl.when(newest >= RUN - REACH)
        def _():
            side_copy(1, newest).start()

    for k in range(REACH):
        side_copy(0, k).wait_recv()
        side_copy(1, k + 1).wait_recv()

    @pl.loop(0, RUN)
    def _(r):
        newest = received(r)
        for j in range(2, 4):
            in_wait(newest, j)

        @pl.loop(0, SPAN)
        def _(o):
            wide_score(newest, newest + o)

    for side in range(2):
        for p in range(REACH):
            put(stat_out.at[side, p], merge(local_parts(p + (REACH + RUN) * side)))
        wstat_copy(side).start()

    lone_score(REACH, 1, 1)
    forward(1)
    lone_score(REACH - 1, 2, 2)

    for side in range(2):
        wstat_copy(side).wait_recv()
    for a in range(RUN):
        parts = local_parts(REACH + a)
        if a < REACH:
            parts.append((stat_in[0, a, 0:thirds, :], stat_in[0, a, thirds : 2 * thirds, :]))
        if a >= RUN - REACH:
            b = a - (RUN - REACH)
            parts.append((stat_in[1, b, 0:thirds, :], stat_in[1, b, thirds : 2 * thirds, :]))
        put(wres.at[REACH + a], merge(parts))
    for side in range(2):
        wres_copy(side).start()

    forward(2)
    lone_score(REACH - 2, 4, 2)

    for side in range(2):
        wres_copy(side).wait_recv()

    def home_round(kind, r):
        h = received(r)
        arrived(kind, h)
        spread(kind, h)

    wide_gradients(zl)
    forward(3)
    lone_score(0, SPAN - 1, 2)
    wide_gradients(lax.rem(zl + 1, RUN))
    lone_combine()
    home_round(1, 0)
    home_round(2, 0)
    wide_gradients(lax.rem(zl + 2, RUN))
    home_round(1, 1)
    home_round(2, 1)
    wide_gradients(lax.rem(zl + 3, RUN))
    send_edge(0)
    send_edge(1)
    lone_gradients()
    home_round(1, 2)
    home_round(2, 2)
    pass_on(1)

    for side in range(2):
        edge_copy(side).wait_recv()
    for a in range(RUN):
        total = wdq[REACH + a]
        if a < REACH:
            total = total + edge_in[0, a].astype(jnp.float32)
        if a >= RUN - REACH:
            total = total + edge_in[1, a - (RUN - REACH)].astype(jnp.float32)
        made[0, a] = (total * scale).T.astype(jnp.bfloat16)
    for r in range(RUN):
        go_home(0, lax.rem(zl + r, RUN))

    pass_on(2)
    home_round(1, 3)
    home_round(2, 3)
    for r in range(RUN):
        home_round(0, r)
    lone_finish()

    for r in range(RUN):
        for j in range(4):
            if r > 0:
                in_copy(r, j).wait_send()
            else:
                @pl.when(jnp.logical_not(stays))
                def _():
                    in_copy(0, j).wait_send()
    for side in range(2):
        for a in range(REACH):
            side_copy(side, a + side).wait_send()
        wstat_copy(side).wait_send()
        wres_copy(side).wait_send()
        edge_copy(side).wait_send()
    for kind in range(3):
        for i in range(RUN):
            @pl.when(jnp.logical_not(jnp.logical_and(stays, zl == i)))
            def _():
                home_copy(kind, i).wait_send()
    for direction in range(2):
        for distance in range(REACH):
            relay(direction, distance).wait_send()
            hop(direction, distance).wait_send()
    for p in range(SPAN):
        if p != REACH:
            stat_copy(p).wait_send()
            res_copy(p).wait_send()
    for kind, target in enumerate(targets):
        for h in range(heads):
            own_part(kind, h).wait()
        others = target.at[0, :, pl.ds(0, (n_head - 1) * heads * DH)]
        pltpu.make_async_copy(others, others, out_send.at[kind]).wait()
        pltpu.make_async_copy(others, others, out_recv.at[kind]).wait()


def copy_kernel(a, b, c, a_out, b_out, c_out, sems):
    copies = [
        pltpu.make_async_copy(source, target, sems.at[i])
        for i, (source, target) in enumerate(((a, a_out), (b, b_out), (c, c_out)))
    ]
    for copy in copies:
        copy.start()
    for copy in copies:
        copy.wait()


def shards(queries, keys, values, grad_out, key_tiles, tile_slot):
    tile, width = queries.shape
    heads = width // DH
    n_ctx = lax.axis_size("ctx")
    n_head = lax.axis_size("head")
    rows = tile // n_head
    lines = 2 * (tile // 128)
    bf16, f32 = jnp.bfloat16, jnp.float32
    dma, vmem, smem = pltpu.SemaphoreType.DMA, pltpu.VMEM, pltpu.SMEM
    out = jax.ShapeDtypeStruct((1, rows, n_head * width), bf16)
    pairs = heads * SPAN * tile * tile
    grads = pl.pallas_call(
        functools.partial(kernel, n_ctx, n_head, heads, tile),
        out_shape=(out, out, out),
        in_specs=[pl.BlockSpec(memory_space=pl.ANY)] * 5,
        out_specs=tuple([pl.BlockSpec(memory_space=pltpu.VMEM)] * 3),
        scratch_shapes=[
            smem(key_tiles.shape[::-1], jnp.int32),
            smem((2, SPAN), f32),
            smem((RUN, SPAN), f32),
            vmem((WIDE, 2, tile, DH), bf16),
            vmem((RUN, 2, tile, DH), bf16),
            vmem((RUN, SPAN, tile, tile), f32),
            vmem((RUN, SPAN, tile, tile), f32),
            vmem((RUN, SPAN, 1, tile), f32),
            vmem((RUN, SPAN, lines, 128), f32),
            vmem((2, REACH, lines, 128), f32),
            vmem((2, REACH, lines, 128), f32),
            vmem((WIDE, lines, 128), f32),
            vmem((WIDE, DH, tile), f32),
            vmem((2, REACH, DH, tile), bf16),
            vmem((2, REACH, DH, tile), bf16),
            vmem((3, RUN, tile, DH), bf16),
            vmem((SPAN, 2, tile, DH), bf16),
            vmem((2, tile, DH), bf16),
            vmem((SPAN, tile, tile), f32),
            vmem((SPAN, tile, tile), f32),
            vmem((SPAN, 1, tile), f32),
            vmem((SPAN, lines, 128), f32),
            vmem((SPAN, lines, 128), f32),
            vmem((lines, 128), f32),
            vmem((SPAN, lines, 128), f32),
            vmem((SPAN, DH, tile), f32),
            vmem((2, REACH, DH, tile), bf16),
            vmem((2, REACH, DH, tile), bf16),
            vmem((heads, tile, DH), bf16),
            vmem((heads, tile, DH), bf16),
            vmem((heads, tile, DH), bf16),
            dma,
            dma((4,)),
            dma((RUN, 4)),
            dma((RUN, 4)),
            dma((2, REACH)),
            dma((2, REACH)),
            dma((2,)),
            dma((2,)),
            dma((2,)),
            dma((2,)),
            dma((2,)),
            dma((2,)),
            dma((3, RUN)),
            dma((3, RUN)),
            dma((2, REACH)),
            dma((2, REACH)),
            dma((SPAN,)),
            dma((SPAN,)),
            dma((SPAN,)),
            dma((SPAN,)),
            dma((2, REACH)),
            dma((2, REACH)),
            dma((3,)),
            dma((3,)),
            dma((3, heads)),
        ],
        compiler_params=pltpu.CompilerParams(
            collective_id=0, has_side_effects=True, vmem_limit_bytes=62 * 1024 * 1024
        ),
        cost_estimate=pl.CostEstimate(
            flops=10 * pairs * DH, bytes_accessed=8 * tile * width * 2, transcendentals=pairs
        ),
    )(key_tiles.T, queries, keys, values, grad_out)
    return pl.pallas_call(
        copy_kernel,
        out_shape=(out, out, out),
        in_specs=[pl.BlockSpec(memory_space=pltpu.VMEM)] * 3,
        out_specs=tuple([pl.BlockSpec(memory_space=pl.ANY)] * 3),
        scratch_shapes=[dma((3,))],
    )(*grads)


def solution(mesh):
    in_specs = (P("ctx", "head"), P("ctx", "head"), P("ctx", "head"), P("ctx", "head"), P(), P())
    out_specs = (P("ctx", "head", None), P("ctx", "head", None), P("ctx", "head", None))
    return jax.shard_map(shards, mesh=mesh, in_specs=in_specs, out_specs=out_specs, check_vma=False)
```

time: 481 us -> 122 us (0.25)
  the two profiles are of different devices: /device:TPU:38 before, /device:TPU:1 now
where the time goes in v3:
time: 122 us
  Pallas kernels  121 us (99%)
    pallas_call x1, Pallas kernels, shards(): pl.pallas_call(functools.partial(kernel, n_ctx, n_head, heads, tile), out...  119 us
    pallas_call x1, Pallas kernels, shards(): pl.pallas_call(copy_kernel, out_shape=(out, out, out), in_specs=[pl.Block...  2.45 us

profile of v3, /device:TPU:1, one launch (start us, length us, event | category | flops | bytes accessed | tf_op | source)
XLA Modules:
  0.0 121.9 jit_solution(603833253838119451)
XLA Ops:
  0.6 118.8 %shard_map.76 = (bf16[1,48,5120]{2,1,0:T(8,128)(2,1)}, bf16[1,48,5120]{2,1,0:T(8,128)(2,1)}, bf16[1,48,5120]{2,1,0:T(8,128)(2,1)}) custom-call(s32[6,32]{1,0:T(8,128)} %bitcast.1, bf16[384,640]{1,0:T(8,128)(2,1)} %q_hbm.1, bf16[384,640]{1,0:T(8,128)(2,1)} %k_hbm.1, bf16[384,640]{1,0:T(8,128)(2,1)} %v_hbm.1, bf16[384,640]{1,0:T(8,128)(2,1)} %g_hbm.1), custom_call_target="tpu_custom_call" | custom-call | flops 6606028800 | bytes 3932160 | tf_op jit(solution)/shard_map/pallas_call | solution.py:627
  119.4 2.5 %shard_map.77 = (bf16[1,48,5120]{2,1,0:T(8,128)(2,1)}, bf16[1,48,5120]{2,1,0:T(8,128)(2,1)}, bf16[1,48,5120]{2,1,0:T(8,128)(2,1)}) custom-call(bf16[1,48,5120]{2,1,0:T(8,128)(2,1)} %get-tuple-element.6.a, bf16[1,48,5120]{2,1,0:T(8,128)(2,1)} %get-tuple-element.7.b, bf16[1,48,5120]{2,1,0:T(8,128)(2,1)} %get-tuple-element.8.c), custom_call_target="tpu_custom_call" | custom-call | tf_op jit(solution)/shard_map/pallas_call | solution.py:697

commit v4 on v3

--- a/solution.py
+++ b/solution.py
@@ -14,6 +14,7 @@
 LOW = -1e30
 MESH = pl.DeviceIdType.MESH
 NT = (((1,), (1,)), ((), ()))
+QUERY_SIDE, KEY_SIDE = (0, 1), (2, 3)
 RING = 8
 RUN = RING // 2
 WIDE = RUN + 2 * REACH
@@ -24,11 +25,11 @@
     tiles_hbm, q_hbm, k_hbm, v_hbm, g_hbm,
     dq_out, dk_out, dv_out,
     tiles_ref, bias, wide_bias,
-    wwin, wkv, wexp, wdp, wtop, wstat, stat_out, stat_in, wres, wdq, edge_out, edge_in, made,
+    wwin, wkv, wexp, wdp, wtop, wstat, part_stat, edge_stat, own_stat, far_stat, wres, wdq, edge_out, edge_in, made,
     win, kv, expon, dprob, summit, lone_out, lone_in, res_out, res_in, part, hop_out, hop_in,
     block_q, block_k, block_v,
     tiles_sem, load_sem, in_send, in_recv, side_send, side_recv, wstat_send, wstat_recv,
-    wres_send, wres_recv, edge_send, edge_recv, home_send, home_recv,
+    edge_send, edge_recv, home_send, home_recv,
     win_send, win_recv, stat_send, stat_recv, res_send, res_recv, hop_send, hop_recv,
     out_send, out_recv, own_sem,
 ):
@@ -56,6 +57,11 @@
         (chip_lane + 1 - core, lax.rem(me + core * RING, n_ctx)),
     )
 
+    far_sides = (
+        (lane, lax.rem(me - RING + n_ctx, n_ctx)),
+        (lane, lax.rem(me + RING, n_ctx)),
+    )
+
     def at(offset):
         return (lane, lax.rem(me + offset + n_ctx, n_ctx))
 
@@ -74,7 +80,7 @@
         @pl.when(jnp.logical_not(jnp.logical_and(stays, zl == i)))
         def _():
             greet(peer(i))
-    for device in sides:
+    for device in sides + far_sides:
         greet(device)
     for offset in range(-REACH, REACH + 1):
         if offset != 0:
@@ -130,11 +136,11 @@
         return jnp.where(found, 0.0, LOW)
 
     pl.semaphore_wait(
-        barrier, 2 + 2 * REACH + n_head - 1 + RUN - jnp.where(stays, 1, 0).astype(jnp.int32)
+        barrier, 4 + 2 * REACH + n_head - 1 + RUN - jnp.where(stays, 1, 0).astype(jnp.int32)
     )
 
-    for r, j in [(r, j) for pair in ((0, 1), (2, 3)) for r in range(RUN) for j in pair]:
-        if True:
+    def send_in(r, pair):
+        for j in pair:
             if r > 0:
                 in_copy(r, j).start()
             else:
@@ -208,23 +214,18 @@
             device_id_type=MESH,
         )
 
-    def wstat_copy(side):
-        return pltpu.make_async_remote_copy(
-            src_ref=stat_out.at[side],
-            dst_ref=stat_in.at[1 - side],
-            send_sem=wstat_send.at[side],
-            recv_sem=wstat_recv.at[1 - side],
-            device_id=sides[side],
-            device_id_type=MESH,
-        )
-
-    def wres_copy(side):
-        return pltpu.make_async_remote_copy(
-            src_ref=wres.at[pl.ds(REACH + side, REACH)],
-            dst_ref=wres.at[pl.ds(REACH + RUN if side == 0 else 0, REACH)],
-            send_sem=wres_send.at[side],
-            recv_sem=wres_recv.at[1 - side],
-            device_id=sides[side],
+    def wstat_copy(side, what):
+        first, count, inbox, device = (
+            (WIDE - REACH if side else 0, REACH, edge_stat, sides[side]),
+            (REACH, RUN, own_stat, sides[side]),
+            (WIDE - REACH if side else 0, REACH, far_stat, far_sides[side]),
+        )[what]
+        return pltpu.make_async_remote_copy(
+            src_ref=part_stat.at[pl.ds(first, count)],
+            dst_ref=inbox.at[1 - side],
+            send_sem=wstat_send.at[side, what],
+            recv_sem=wstat_recv.at[1 - side, what],
+            device_id=device,
             device_id_type=MESH,
         )
 
@@ -371,7 +372,7 @@
             return carry[0] + dk, carry[1] + dv
 
         start = (jnp.zeros((tile, DH), jnp.float32), jnp.zeros((tile, DH), jnp.float32))
-        dk, dv = lax.fori_loop(0, SPAN, body, start)
+        dk, dv = lax.fori_loop(0, SPAN, body, start, unroll=SPAN)
         made[1, i] = (dk * scale).astype(jnp.bfloat16)
         made[2, i] = dv.astype(jnp.bfloat16)
         go_home(1, i)
@@ -383,7 +384,7 @@
         edge_copy(side).start()
 
     def lone_score(first, stride, count):
-        @pl.loop(0, count)
+        @pl.loop(0, count, unroll=count)
         def _(i):
             p = first + stride * i
             score(
@@ -427,7 +428,7 @@
             return carry[0] + dk, carry[1] + dv
 
         start = (jnp.zeros((tile, DH), jnp.float32), jnp.zeros((tile, DH), jnp.float32))
-        dk, dv = lax.fori_loop(0, SPAN, body, start)
+        dk, dv = lax.fori_loop(0, SPAN, body, start, unroll=SPAN)
         for direction, p in ((0, 0), (1, 2 * REACH)):
             hop_out[direction, 0] = part[p].astype(jnp.bfloat16)
             hop(direction, 0).start()
@@ -452,11 +453,103 @@
         block_q[last] = (total * scale).T.astype(jnp.bfloat16)
         spread(0, last)
 
+    def received(r):
+        return lax.rem(zl - r + RUN, RUN)
+
+    def take_tiles(r):
+        newest = received(r)
+        for j in QUERY_SIDE:
+            in_wait(newest, j)
+
+        @pl.when(newest < REACH)
+        def _():
+            side_copy(0, newest).start()
+
+        @pl.when(newest >= RUN - REACH)
+        def _():
+            side_copy(1, newest).start()
+
+    def wait_sides():
+        for k in range(REACH):
+            side_copy(0, k).wait_recv()
+            side_copy(1, k + 1).wait_recv()
+
+    def take_keys(first, count):
+        @pl.loop(first, first + count)
+        def _(r):
+            newest = received(r)
+            for j in KEY_SIDE:
+                in_wait(newest, j)
+
+            @pl.loop(0, SPAN, unroll=SPAN)
+            def _(o):
+                wide_score(newest, newest + o)
+
+    def send_stats():
+        for p in range(WIDE):
+            put(part_stat.at[p], merge(local_parts(p)))
+        for side in range(2):
+            for what in range(3):
+                wstat_copy(side, what).start()
+
+    def wide_combine():
+        for side in range(2):
+            for what in range(3):
+                wstat_copy(side, what).wait_recv()
+
+        def read(ref, *index):
+            return (
+                ref[(*index, slice(0, thirds), slice(None))],
+                ref[(*index, slice(thirds, 2 * thirds), slice(None))],
+            )
+
+        for p in range(WIDE):
+            parts = [read(part_stat, p)]
+            a = p - REACH
+            if a < 0:
+                parts.append(read(own_stat, 0, a + RUN))
+                if a + RUN < REACH:
+                    parts.append(read(far_stat, 0, a + RUN))
+            elif a >= RUN:
+                parts.append(read(own_stat, 1, a - RUN))
+                if a - RUN >= RUN - REACH:
+                    parts.append(read(far_stat, 1, a - RUN - (RUN - REACH)))
+            else:
+                if a < REACH:
+                    parts.append(read(edge_stat, 0, a))
+                if a >= RUN - REACH:
+                    parts.append(read(edge_stat, 1, a - (RUN - REACH)))
+            put(wres.at[p], merge(parts))
+
+    def home_round(kind, r):
+        h = received(r)
+        arrived(kind, h)
+        spread(kind, h)
+
+    def wide_round(r):
+        wide_gradients(lax.rem(zl + r, RUN))
+
+    def finish_queries():
+        for side in range(2):
+            edge_copy(side).wait_recv()
+        for a in range(RUN):
+            total = wdq[REACH + a]
+            if a < REACH:
+                total = total + edge_in[0, a].astype(jnp.float32)
+            if a >= RUN - REACH:
+                total = total + edge_in[1, a - (RUN - REACH)].astype(jnp.float32)
+            made[0, a] = (total * scale).T.astype(jnp.bfloat16)
+        for r in range(RUN):
+            go_home(0, lax.rem(zl + r, RUN))
+
     for copy in loads:
         copy.wait()
+    send_in(0, QUERY_SIDE)
+    send_in(1, QUERY_SIDE)
     for direction in range(2):
         relay(direction, 0).start()
-
+    send_in(2, QUERY_SIDE)
+    send_in(3, QUERY_SIDE)
     wdq[...] = jnp.zeros_like(wdq)
     for p in range(SPAN):
         other = lax.rem(me + p - REACH + n_ctx, n_ctx)
@@ -466,105 +559,50 @@
         for o in range(SPAN):
             query_tile = lax.rem(first_tile + i + o - REACH + n_ctx, n_ctx)
             wide_bias[i, o] = listed(query_tile, first_tile + i)
-
-    def received(r):
-        return lax.rem(zl - r + RUN, RUN)
-
-    for r in range(RUN):
-        newest = received(r)
-        for j in range(2):
-            in_wait(newest, j)
-
-        @pl.when(newest < REACH)
-        def _():
-            side_copy(0, newest).start()
-
-        @pl.when(newest >= RUN - REACH)
-        def _():
-            side_copy(1, newest).start()
-
-    for k in range(REACH):
-        side_copy(0, k).wait_recv()
-        side_copy(1, k + 1).wait_recv()
-
-    @pl.loop(0, RUN)
-    def _(r):
-        newest = received(r)
-        for j in range(2, 4):
-            in_wait(newest, j)
-
-        @pl.loop(0, SPAN)
-        def _(o):
-            wide_score(newest, newest + o)
-
-    for side in range(2):
-        for p in range(REACH):
-            put(stat_out.at[side, p], merge(local_parts(p + (REACH + RUN) * side)))
-        wstat_copy(side).start()
-
-    lone_score(REACH, 1, 1)
+    take_tiles(0)
+    take_tiles(1)
     forward(1)
-    lone_score(REACH - 1, 2, 2)
-
-    for side in range(2):
-        wstat_copy(side).wait_recv()
-    for a in range(RUN):
-        parts = local_parts(REACH + a)
-        if a < REACH:
-            parts.append((stat_in[0, a, 0:thirds, :], stat_in[0, a, thirds : 2 * thirds, :]))
-        if a >= RUN - REACH:
-            b = a - (RUN - REACH)
-            parts.append((stat_in[1, b, 0:thirds, :], stat_in[1, b, thirds : 2 * thirds, :]))
-        put(wres.at[REACH + a], merge(parts))
-    for side in range(2):
-        wres_copy(side).start()
-
+    send_in(0, KEY_SIDE)
+    send_in(1, KEY_SIDE)
+    send_in(2, KEY_SIDE)
+    send_in(3, KEY_SIDE)
+    lone_score(REACH - 1, 1, 3)
+    take_tiles(2)
+    take_tiles(3)
     forward(2)
     lone_score(REACH - 2, 4, 2)
-
-    for side in range(2):
-        wres_copy(side).wait_recv()
-
-    def home_round(kind, r):
-        h = received(r)
-        arrived(kind, h)
-        spread(kind, h)
-
-    wide_gradients(zl)
+    wait_sides()
+    take_keys(0, 1)
+    take_keys(1, 1)
+    take_keys(2, 1)
+    take_keys(3, 1)
+    send_stats()
     forward(3)
     lone_score(0, SPAN - 1, 2)
-    wide_gradients(lax.rem(zl + 1, RUN))
+    wide_combine()
+    wide_round(0)
     lone_combine()
+    wide_round(1)
+    wide_round(2)
+    lone_gradients()
+    wide_round(3)
+    send_edge(0)
+    send_edge(1)
     home_round(1, 0)
     home_round(2, 0)
-    wide_gradients(lax.rem(zl + 2, RUN))
+    pass_on(1)
     home_round(1, 1)
     home_round(2, 1)
-    wide_gradients(lax.rem(zl + 3, RUN))
-    send_edge(0)
-    send_edge(1)
-    lone_gradients()
+    finish_queries()
+    pass_on(2)
     home_round(1, 2)
     home_round(2, 2)
-    pass_on(1)
-
-    for side in range(2):
-        edge_copy(side).wait_recv()
-    for a in range(RUN):
-        total = wdq[REACH + a]
-        if a < REACH:
-            total = total + edge_in[0, a].astype(jnp.float32)
-        if a >= RUN - REACH:
-            total = total + edge_in[1, a - (RUN - REACH)].astype(jnp.float32)
-        made[0, a] = (total * scale).T.astype(jnp.bfloat16)
-    for r in range(RUN):
-        go_home(0, lax.rem(zl + r, RUN))
-
-    pass_on(2)
     home_round(1, 3)
     home_round(2, 3)
-    for r in range(RUN):
-        home_round(0, r)
+    home_round(0, 0)
+    home_round(0, 1)
+    home_round(0, 2)
+    home_round(0, 3)
     lone_finish()
 
     for r in range(RUN):
@@ -578,8 +616,8 @@
     for side in range(2):
         for a in range(REACH):
             side_copy(side, a + side).wait_send()
-        wstat_copy(side).wait_send()
-        wres_copy(side).wait_send()
+        for what in range(3):
+            wstat_copy(side, what).wait_send()
         edge_copy(side).wait_send()
     for kind in range(3):
         for i in range(RUN):
@@ -639,7 +677,9 @@
             vmem((RUN, SPAN, tile, tile), f32),
             vmem((RUN, SPAN, 1, tile), f32),
             vmem((RUN, SPAN, lines, 128), f32),
+            vmem((WIDE, lines, 128), f32),
             vmem((2, REACH, lines, 128), f32),
+            vmem((2, RUN, lines, 128), f32),
             vmem((2, REACH, lines, 128), f32),
             vmem((WIDE, lines, 128), f32),
             vmem((WIDE, DH, tile), f32),
@@ -667,10 +707,8 @@
             dma((RUN, 4)),
             dma((2, REACH)),
             dma((2, REACH)),
-            dma((2,)),
-            dma((2,)),
-            dma((2,)),
-            dma((2,)),
+            dma((2, 3)),
+            dma((2, 3)),
             dma((2,)),
             dma((2,)),
             dma((3, RUN)),

time: 122 us -> 112 us (0.918)
  Pallas kernels: 121 us -> 111 us
    pallas_call x1, Pallas kernels: 119 us -> 108 us  [shards(): pl.pallas_call(functools.partial(kernel, n_ctx, n_head, heads, tile), out...]
where the time goes in v4:
time: 112 us; the launch traced here: 111 us
  Pallas kernels  111 us (99%)
    pallas_call x1, Pallas kernels, shards(): pl.pallas_call(functools.partial(kernel, n_ctx, n_head, heads, tile), out...  108 us
    pallas_call x1, Pallas kernels, shards(): pl.pallas_call(copy_kernel, out_shape=(out, out, out), in_specs=[pl.Block...  2.45 us

profile of v4, /device:TPU:1, one launch (start us, length us, event | category | flops | bytes accessed | tf_op | source)
XLA Modules:
  0.0 111.4 jit_solution(16799317051297175573)
XLA Ops:
  0.6 108.1 %shard_map.76 = (bf16[1,48,5120]{2,1,0:T(8,128)(2,1)}, bf16[1,48,5120]{2,1,0:T(8,128)(2,1)}, bf16[1,48,5120]{2,1,0:T(8,128)(2,1)}) custom-call(s32[6,32]{1,0:T(8,128)} %bitcast.1, bf16[384,640]{1,0:T(8,128)(2,1)} %q_hbm.1, bf16[384,640]{1,0:T(8,128)(2,1)} %k_hbm.1, bf16[384,640]{1,0:T(8,128)(2,1)} %v_hbm.1, bf16[384,640]{1,0:T(8,128)(2,1)} %g_hbm.1), custom_call_target="tpu_custom_call" | custom-call | flops 6606028800 | bytes 3932160 | tf_op jit(solution)/shard_map/pallas_call | solution.py:665
  108.8 2.5 %shard_map.77 = (bf16[1,48,5120]{2,1,0:T(8,128)(2,1)}, bf16[1,48,5120]{2,1,0:T(8,128)(2,1)}, bf16[1,48,5120]{2,1,0:T(8,128)(2,1)}) custom-call(bf16[1,48,5120]{2,1,0:T(8,128)(2,1)} %get-tuple-element.6.a, bf16[1,48,5120]{2,1,0:T(8,128)(2,1)} %get-tuple-element.7.b, bf16[1,48,5120]{2,1,0:T(8,128)(2,1)} %get-tuple-element.8.c), custom_call_target="tpu_custom_call" | custom-call | tf_op jit(solution)/shard_map/pallas_call | solution.py:735

commit v5 on v4

--- a/solution.py
+++ b/solution.py
@@ -582,21 +582,21 @@
     wide_combine()
     wide_round(0)
     lone_combine()
+    wide_round(2)
     wide_round(1)
-    wide_round(2)
     lone_gradients()
     wide_round(3)
     send_edge(0)
     send_edge(1)
+    pass_on(1)
     home_round(1, 0)
     home_round(2, 0)
-    pass_on(1)
+    home_round(1, 2)
+    home_round(2, 2)
+    finish_queries()
     home_round(1, 1)
     home_round(2, 1)
-    finish_queries()
     pass_on(2)
-    home_round(1, 2)
-    home_round(2, 2)
     home_round(1, 3)
     home_round(2, 3)
     home_round(0, 0)

time: 112 us -> 112 us (level)
  no operation moved by 1% of the time
where the time goes in v5:
time: 112 us
  Pallas kernels  111 us (99%)
    pallas_call x1, Pallas kernels, shards(): pl.pallas_call(functools.partial(kernel, n_ctx, n_head, heads, tile), out...  109 us
    pallas_call x1, Pallas kernels, shards(): pl.pallas_call(copy_kernel, out_shape=(out, out, out), in_specs=[pl.Block...  2.45 us

profile of v5, /device:TPU:1, one launch (start us, length us, event | category | flops | bytes accessed | tf_op | source)
XLA Modules:
  0.0 112.3 jit_solution(5034544848904485016)
XLA Ops:
  0.6 109.0 %shard_map.76 = (bf16[1,48,5120]{2,1,0:T(8,128)(2,1)}, bf16[1,48,5120]{2,1,0:T(8,128)(2,1)}, bf16[1,48,5120]{2,1,0:T(8,128)(2,1)}) custom-call(s32[6,32]{1,0:T(8,128)} %bitcast.1, bf16[384,640]{1,0:T(8,128)(2,1)} %q_hbm.1, bf16[384,640]{1,0:T(8,128)(2,1)} %k_hbm.1, bf16[384,640]{1,0:T(8,128)(2,1)} %v_hbm.1, bf16[384,640]{1,0:T(8,128)(2,1)} %g_hbm.1), custom_call_target="tpu_custom_call" | custom-call | flops 6606028800 | bytes 3932160 | tf_op jit(solution)/shard_map/pallas_call | solution.py:665
  109.6 2.5 %shard_map.77 = (bf16[1,48,5120]{2,1,0:T(8,128)(2,1)}, bf16[1,48,5120]{2,1,0:T(8,128)(2,1)}, bf16[1,48,5120]{2,1,0:T(8,128)(2,1)}) custom-call(bf16[1,48,5120]{2,1,0:T(8,128)(2,1)} %get-tuple-element.6.a, bf16[1,48,5120]{2,1,0:T(8,128)(2,1)} %get-tuple-element.7.b, bf16[1,48,5120]{2,1,0:T(8,128)(2,1)} %get-tuple-element.8.c), custom_call_target="tpu_custom_call" | custom-call | tf_op jit(solution)/shard_map/pallas_call | solution.py:735
